TPU v7x, 32 devices: a whole 2x2x4 slice. The times are simulated.
32 devices in a mesh: dp: 16 (over z, y, core), tensor: 2 (over x).
Axes of the slice: x: 2, y: 2, z: 4, core: 2. Of those that a mesh axis runs over, the one named last changes fastest.
Arguments:
- inputs: bfloat16 [73728, 512], P(('dp', 'tensor')), may hold values from -3 to 3
- pack_long: int32 [192], P('dp'), may hold values from 0 to 1
- item_table: int32 [768], P('dp'), may hold values from 0 to 63
- tau_table: float32 [64], replicated, may hold values from 0.5 to 2
- delta_table: float32 [64, 384], replicated, may hold values from -6 to 6
- project_weight: bfloat16 [3, 512, 512], P(None, None, 'tensor'), may hold values from -0.25 to 0.25
- project_bias: float32 [2, 512], P(None, 'tensor'), may hold values from -1.5 to 1.5
- merge_weight: bfloat16 [512, 512], P('tensor'), may hold values from -1 to 1
- merge_bias: float32 [512], replicated, may hold values from -1.5 to 1.5
- first_gain: float32 [512], replicated, may hold values from 0.5 to 1.5
- first_shift: float32 [512], replicated, may hold values from -1 to 1
- expand_weight: bfloat16 [512, 2048], P(None, 'tensor'), may hold values from -0.25 to 0.25
- expand_bias: float32 [2048], P('tensor'), may hold values from -1.5 to 1.5
- reduce_weight: bfloat16 [2048, 512], P('tensor'), may hold values from -0.25 to 0.25
- reduce_bias: float32 [512], replicated, may hold values from -1.5 to 1.5
- second_gain: float32 [512], replicated, may hold values from 0.5 to 1.5
- second_shift: float32 [512], replicated, may hold values from -1 to 1
- grad_output: bfloat16 [73728, 512], P(('dp', 'tensor')), may hold values from -3 to 3
Outputs:
- block_output: float32 [73728, 512], P(('dp', 'tensor'))
- input_grad: float32 [73728, 512], P(('dp', 'tensor'))
- project_weight_grad: float32 [3, 512, 512], P(None, None, 'tensor')
- project_bias_grad: float32 [2, 512], P(None, 'tensor')
- merge_weight_grad: float32 [512, 512], P('tensor')
- merge_bias_grad: float32 [512], replicated
- first_gain_grad: float32 [512], replicated
- first_shift_grad: float32 [512], replicated
- expand_weight_grad: float32 [512, 2048], P(None, 'tensor')
- expand_bias_grad: float32 [2048], P('tensor')
- reduce_weight_grad: float32 [2048, 512], P('tensor')
- reduce_bias_grad: float32 [512], replicated
- second_gain_grad: float32 [512], replicated
- second_shift_grad: float32 [512], replicated
All inputs are finite; a program needn't handle non-finite values.
Results may differ from a plain program's by a relative error of at most 0.02.
The roundings to bfloat16 on the way count: a program that leaves them out, or rounds other values in their place, can miss the bound.
Values may be sent and summed in bfloat16 or wider, within the bound.
No kernel may reach another device: no remote copies, remote signals or barrier semaphores. Data moves between devices by JAX's collectives and lax.ppermute only.
A program may use at most 192 MiB of HBM per device.

v0:
```python
import jax
import jax.numpy as jnp
from jax import lax
from jax.sharding import PartitionSpec as P

HEAD = 64
SHORT = 96
LONG = 384
TABLE = 64


def layer_norm(values, gain, shift):
    mean = jnp.mean(values, axis=-1, keepdims=True)
    centred = values - mean
    spread = jnp.mean(centred * centred, axis=-1, keepdims=True)
    return centred * lax.rsqrt(spread + 1e-05) * gain + shift


def exact_gelu(values):
    return jax.nn.gelu(values, approximate=False)


def describe(pack_long, item_table, tau_table, delta_table):
    packs = pack_long.shape[0]
    per = LONG // SHORT
    count = packs * LONG
    longer = jnp.broadcast_to(pack_long[:, None] == 1, (packs, LONG)).reshape(count)
    lead_row = jnp.broadcast_to(item_table.reshape(packs, per)[:, :1], (packs, LONG)).reshape(count)
    each_row = jnp.broadcast_to(item_table[:, None], (packs * per, SHORT)).reshape(count)
    table_row = jnp.where(longer, lead_row, each_row)
    places = jnp.arange(count, dtype=jnp.int32)
    position = jnp.where(longer, places % LONG, places % SHORT)
    segment = jnp.where(longer, places // LONG * per, places // SHORT)
    picker = (table_row[:, None] == jnp.arange(TABLE, dtype=jnp.int32)[None, :]).astype(jnp.float32)
    tau_row = jnp.sum(picker * tau_table[None, :], axis=1)
    picked = jnp.dot(
        picker, delta_table, precision=lax.Precision.HIGHEST, preferred_element_type=jnp.float32
    )
    placed = position[:, None] == jnp.arange(LONG, dtype=jnp.int32)[None, :]
    delta_row = jnp.sum(jnp.where(placed, picked, 0.0), axis=1)
    return (tau_row, delta_row, segment)


def project(rows_all, project_weight, project_bias):
    query = (
        jnp.dot(rows_all, project_weight[0], preferred_element_type=jnp.float32) + project_bias[0]
    ).astype(jnp.bfloat16)
    keys = jnp.dot(rows_all, project_weight[1], preferred_element_type=jnp.float32).astype(
        jnp.bfloat16
    )
    values = (
        jnp.dot(rows_all, project_weight[2], preferred_element_type=jnp.float32) + project_bias[1]
    ).astype(jnp.bfloat16)
    return (query, keys, values)


def split_blocks(arrays):
    width = 2 * LONG
    return tuple((a.reshape((a.shape[0] // width, width) + a.shape[1:]) for a in arrays))


def block_scores(block_q, block_k, block_tau, block_delta, block_seg):
    raw = jnp.einsum("qhd,khd->hqk", block_q, block_k, preferred_element_type=jnp.float32)
    scores = (block_tau[None, :, None] * raw + block_delta[None, None, :]) * HEAD ** (-0.5)
    same = block_seg[:, None] == block_seg[None, :]
    return jnp.where(same[None], scores, -1e30)


def attend_forward(query, keys, values, tau_row, delta_row, segment):
    heads = query.shape[1] // HEAD
    shaped = tuple((a.reshape(a.shape[0], heads, HEAD) for a in (query, keys, values)))

    def one_block(parts):
        block_q, block_k, block_v, block_tau, block_delta, block_seg = parts
        scores = block_scores(block_q, block_k, block_tau, block_delta, block_seg)
        top = jnp.max(scores, axis=-1, keepdims=True)
        expo = jnp.exp(scores - top)
        totals = jnp.sum(expo, axis=-1, keepdims=True)
        weights = (expo / totals).astype(jnp.bfloat16)
        mixed = jnp.einsum("hqk,khd->qhd", weights, block_v, preferred_element_type=jnp.float32)
        return (
            mixed.reshape(mixed.shape[0], heads * HEAD).astype(jnp.bfloat16),
            top + jnp.log(totals),
        )

    attended, logsum = lax.map(one_block, split_blocks(shaped + (tau_row, delta_row, segment)))
    return (attended.reshape(query.shape), logsum)


def attend_backward(query, keys, values, grad_att, logsum, tau_row, delta_row, segment):
    heads = query.shape[1] // HEAD
    shaped = tuple((a.reshape(a.shape[0], heads, HEAD) for a in (query, keys, values, grad_att)))
    blocked = split_blocks(shaped + (tau_row, delta_row, segment))

    def one_block(parts):
        block_q, block_k, block_v, block_g, block_lse, block_tau, block_delta, block_seg = parts
        scores = block_scores(block_q, block_k, block_tau, block_delta, block_seg)
        probs = jnp.exp(scores - block_lse)
        dprob = jnp.einsum("qhd,khd->hqk", block_g, block_v, preferred_element_type=jnp.float32)
        dscore = probs * (dprob - jnp.sum(dprob * probs, axis=-1, keepdims=True))
        lowered = (dscore * HEAD ** (-0.5) * block_tau[None, :, None]).astype(jnp.bfloat16)
        grad_q = jnp.einsum("hqk,khd->qhd", lowered, block_k, preferred_element_type=jnp.float32)
        grad_k = jnp.einsum("hqk,qhd->khd", lowered, block_q, preferred_element_type=jnp.float32)
        grad_v = jnp.einsum(
            "hqk,qhd->khd", probs.astype(jnp.bfloat16), block_g, preferred_element_type=jnp.float32
        )
        width = block_q.shape[0]
        return tuple(
            (g.reshape(width, heads * HEAD).astype(jnp.bfloat16) for g in (grad_q, grad_k, grad_v))
        )

    grads = lax.map(one_block, blocked[:4] + (logsum,) + blocked[4:])
    return tuple((g.reshape(query.shape) for g in grads))


def row_term(left, right, form):
    return jnp.einsum(form, left, right, preferred_element_type=jnp.float32)


def feed_backward(feed_rows, preact_rows, active_rows, grad_fed, reduce_matrix):
    grad_reduce_weight = jnp.einsum(
        "tf,td->fd", active_rows, grad_fed, preferred_element_type=jnp.float32
    )
    grad_active = jnp.einsum(
        "td,fd->tf", grad_fed, reduce_matrix, preferred_element_type=jnp.float32
    )
    grad_preact = jax.vjp(exact_gelu, preact_rows)[1](grad_active)[0].astype(jnp.bfloat16)
    grad_expand_bias = jnp.sum(grad_preact.astype(jnp.float32), axis=0)
    grad_expand_weight = jnp.einsum(
        "td,tf->df", feed_rows, grad_preact, preferred_element_type=jnp.float32
    )
    return (grad_reduce_weight, grad_preact, grad_expand_bias, grad_expand_weight)


def on_device(
    inputs,
    pack_long,
    item_table,
    tau_table,
    delta_table,
    project_weight,
    project_bias,
    merge_weight,
    merge_bias,
    first_gain,
    first_shift,
    expand_weight,
    expand_bias,
    reduce_weight,
    reduce_bias,
    second_gain,
    second_shift,
    grad_output,
):
    tau_row, delta_row, segment = describe(pack_long, item_table, tau_table, delta_table)
    rows_all = lax.all_gather(inputs, "tensor", axis=0, tiled=True)
    query, keys, values = project(rows_all, project_weight, project_bias)
    attended, logsum = attend_forward(query, keys, values, tau_row, delta_row, segment)
    mixed_part = lax.psum_scatter(
        row_term(attended, merge_weight, "tc,cd->td"), "tensor", scatter_dimension=0, tiled=True
    )
    first_sum = inputs.astype(jnp.float32) + (mixed_part + merge_bias)
    normed, first_back = jax.vjp(layer_norm, first_sum, first_gain, first_shift)
    normed_low = normed.astype(jnp.bfloat16)
    feed_all = lax.all_gather(normed_low, "tensor", axis=0, tiled=True)
    preact = jnp.dot(feed_all, expand_weight, preferred_element_type=jnp.float32) + expand_bias
    active = exact_gelu(preact).astype(jnp.bfloat16)
    fed_part = lax.psum_scatter(
        row_term(active, reduce_weight, "tf,fd->td"), "tensor", scatter_dimension=0, tiled=True
    )
    second_sum = normed + (fed_part + reduce_bias)
    block_output, second_back = jax.vjp(layer_norm, second_sum, second_gain, second_shift)
    grad_second, grad_gain_b, grad_shift_b = second_back(grad_output.astype(jnp.float32))
    grad_reduce_bias = jnp.sum(grad_second, axis=0)
    grad_fed = lax.all_gather(grad_second.astype(jnp.bfloat16), "tensor", axis=0, tiled=True)
    feed_again = lax.all_gather(normed_low, "tensor", axis=0, tiled=True)
    preact_again = (
        jnp.dot(feed_again, expand_weight, preferred_element_type=jnp.float32) + expand_bias
    )
    active_again = exact_gelu(preact_again).astype(jnp.bfloat16)
    grad_reduce_weight, grad_preact, grad_expand_bias, grad_expand_weight = feed_backward(
        feed_again, preact_again, active_again, grad_fed, reduce_weight
    )
    grad_normed = grad_second + lax.psum_scatter(
        row_term(grad_preact, expand_weight, "tf,df->td"), "tensor", scatter_dimension=0, tiled=True
    )
    grad_first, grad_gain_a, grad_shift_a = first_back(grad_normed)
    grad_merge_bias = jnp.sum(grad_first, axis=0)
    grad_att = lax.all_gather(grad_first.astype(jnp.bfloat16), "tensor", axis=0, tiled=True)
    grad_merge_weight = jnp.einsum(
        "tc,td->cd", attended, grad_att, preferred_element_type=jnp.float32
    )
    grad_attended = jnp.einsum(
        "td,cd->tc", grad_att, merge_weight, preferred_element_type=jnp.float32
    ).astype(jnp.bfloat16)
    rows_again = lax.all_gather(inputs, "tensor", axis=0, tiled=True)
    query_again, keys_again, values_again = project(rows_again, project_weight, project_bias)
    grad_q, grad_k, grad_v = attend_backward(
        query_again, keys_again, values_again, grad_attended, logsum, tau_row, delta_row, segment
    )
    grad_stack = jnp.stack((grad_q, grad_k, grad_v), axis=1)
    grad_project_weight = jnp.einsum(
        "td,tjc->jdc", rows_again, grad_stack, preferred_element_type=jnp.float32
    )
    grad_project_bias = jnp.stack(
        (jnp.sum(grad_q.astype(jnp.float32), axis=0), jnp.sum(grad_v.astype(jnp.float32), axis=0))
    )
    input_grad = grad_first + lax.psum_scatter(
        row_term(grad_stack, project_weight, "tjc,jdc->td").astype(jnp.bfloat16),
        "tensor",
        scatter_dimension=0,
        tiled=True,
    ).astype(jnp.float32)
    summed_all = (
        lax.psum(grad_project_weight.astype(jnp.bfloat16), "dp").astype(jnp.float32),
        lax.psum(grad_project_bias.astype(jnp.bfloat16), "dp").astype(jnp.float32),
        lax.psum(grad_merge_weight.astype(jnp.bfloat16), "dp").astype(jnp.float32),
        lax.psum(grad_expand_weight.astype(jnp.bfloat16), "dp").astype(jnp.float32),
        lax.psum(grad_expand_bias.astype(jnp.bfloat16), "dp").astype(jnp.float32),
        lax.psum(grad_reduce_weight.astype(jnp.bfloat16), "dp").astype(jnp.float32),
    )
    summed_attention = summed_all[:3]
    summed_feed = summed_all[3:]
    small = lax.psum(
        (grad_merge_bias, grad_gain_a, grad_shift_a, grad_reduce_bias, grad_gain_b, grad_shift_b),
        ("dp", "tensor"),
    )
    return (
        block_output,
        input_grad,
        summed_attention[0],
        summed_attention[1],
        summed_attention[2],
        small[0],
        small[1],
        small[2],
        summed_feed[0],
        summed_feed[1],
        summed_feed[2],
        small[3],
        small[4],
        small[5],
    )


def solution(mesh):
    placed = (
        P(("dp", "tensor"), None),
        P("dp"),
        P("dp"),
        P(),
        P(),
        P(None, None, "tensor"),
        P(None, "tensor"),
        P("tensor", None),
        P(),
        P(),
        P(),
        P(None, "tensor"),
        P("tensor"),
        P("tensor", None),
        P(),
        P(),
        P(),
        P(("dp", "tensor"), None),
    )
    return jax.shard_map(
        on_device,
        mesh=mesh,
        in_specs=placed,
        out_specs=(
            P(("dp", "tensor"), None),
            P(("dp", "tensor"), None),
            P(None, None, "tensor"),
            P(None, "tensor"),
            P("tensor", None),
            P(),
            P(),
            P(),
            P(None, "tensor"),
            P("tensor"),
            P("tensor", None),
            P(),
            P(),
            P(),
        ),
        check_vma=False,
    )
```

profile of v0, /device:TPU:0, one launch (start us, length us, event | category | flops | bytes accessed | tf_op | source)
XLA Modules:
  0.0 1409.9 jit_solution(6680102642306665153)
XLA Ops:
  15.7 59.3 %all-gather.5.cloned.1.call-done = bf16[4608,512]{1,0:T(8,128)(2,1)} async-done(((bf16[2304,512]{1,0:T(8,128)(2,1)}), bf16[4608,512]{1,0:T(8,128)(2,1)}) %all-gather.5.cloned.1.call-update) | async-done | bytes 4718608 | tf_op jit(solution)/shard_map/all_gather | solution.py:156
  122.4 82.6 %while.26 = (s32[]{:T(128)}, bf16[6,768,256]{2,1,0:T(8,128)(2,1)}, f32[6,4,768,1]{2,1,3,0:T(4,128)}, bf16[6,768,4,64]{1,3,2,0:T(8,128)(2,1)}, s32[6,768]{1,0:T(8...) while((s32[]{:T(128)}, bf16[6,768,256]{2,1,0:T(8,128)(2,1)}, ...), condition=%wide.region_5.6_spmd, body=%wide.region_2.5_spmd.sunk | while | flops 647230464 | bytes 33957484 | solution.py:86
  211.9 110.7 %reduce-scatter.5.cloned.1.call-done = f32[2304,512]{1,0:T(8,128)} async-done(((f32[4608,512]{1,0:T(8,128)}), f32[2304,512]{1,0:T(8,128)}) %reduce-scatter.5.cloned.1.call-update) | async-done | bytes 4718608 | tf_op jit(solution)/shard_map/reduce_scatter | solution.py:159
  330.8 62.8 %all-gather.7.cloned.1.call-done = bf16[4608,512]{1,0:T(8,128)(2,1)} async-done(((bf16[2304,512]{1,0:T(8,128)(2,1)}), bf16[4608,512]{1,0:T(8,128)(2,1)}) %all-gather.7.cloned.1.call-update) | async-done | bytes 4718608 | tf_op jit(solution)/shard_map/all_gather | solution.py:165
  393.6 47.4 %multiply_convert_fusion.1 = (bf16[4608,1024]{1,0:T(8,128)(2,1)S(1)}, f32[4608,1024]{1,0:T(8,128)}, f32[4608,1024]{1,0:T(8,128)}) fusion(f32[1024]{0:T(1024)S(1)} %copy-done.41, bf16[4608,512]{1,0:T(8,128)(2,1)} %all-gather.7.cloned.1.call-done, bf16[512,1024]{1,0:T(8,128)(2,1)S(1)} %copy-done), kind=kOutput, calls=%fused_computation.70 | convolution fusion | flops 5143265280 | bytes 52957184 | tf_op jit(solution)/shard_map/dot_general | solution.py:166
  452.3 110.7 %reduce-scatter.7.cloned.1.call-done = f32[2304,512]{1,0:T(8,128)} async-done(((f32[4608,512]{1,0:T(8,128)}), f32[2304,512]{1,0:T(8,128)}) %reduce-scatter.7.cloned.1.call-update) | async-done | bytes 4718608 | tf_op jit(solution)/shard_map/reduce_scatter | solution.py:168
  580.5 62.8 %all-gather.9.cloned.1.call-done = bf16[4608,512]{1,0:T(8,128)(2,1)} async-done(((bf16[2304,512]{1,0:T(8,128)(2,1)}), bf16[4608,512]{1,0:T(8,128)(2,1)}) %all-gather.9.cloned.1.call-update) | async-done | bytes 4718608 | tf_op jit(solution)/shard_map/all_gather | solution.py:175
  643.2 20.8 %fusion.102 = (bf16[1024]{0:T(1024)(128)(2,1)}, bf16[4608,1024]{1,0:T(8,128)(2,1)}) fusion(f32[4608,1024]{1,0:T(8,128)} %get-tuple-element.306, f32[4608,1024]{1,0:T(8,128)} %get-tuple-element.324, f32[1024]{0:T(1024)S(1)} %copy-done.41, bf16[4608,512]{1,0:T(8,128)(2,1)} %all-gather.9.cloned.1.call-done, bf16[1024,512]{1,0:T(8,128)(2,1)S(1)} %copy-done.40), kind=kOutput, calls=%fused_computation.172 | convolution fusion | flops 4907334656 | bytes 52959232 | tf_op jit(solution)/shard_map/td,fd->tf/dot_general | solution.py:124
  664.1 11.3 fusion.111
  675.4 110.6 %reduce-scatter.9.cloned.1.call-done = f32[2304,512]{1,0:T(8,128)} async-done(((f32[4608,512]{1,0:T(8,128)}), f32[2304,512]{1,0:T(8,128)}) %reduce-scatter.9.cloned.1.call-update) | async-done | bytes 4718608 | tf_op jit(solution)/shard_map/reduce_scatter | solution.py:184
  801.0 10.0 convolution_convert_fusion.2
  810.9 9.1 convolution_convert_fusion.3
  820.1 43.6 %all-gather.11.cloned.1.call-done = bf16[4608,512]{1,0:T(8,128)(2,1)} async-done(((bf16[2304,512]{1,0:T(8,128)(2,1)}), bf16[4608,512]{1,0:T(8,128)(2,1)}) %all-gather.11.cloned.1.call-update) | async-done | bytes 4718608 | tf_op jit(solution)/shard_map/all_gather | solution.py:189
  879.4 330.9 %while.27 = (s32[]{:T(128)}, bf16[6,768,256]{1,2,0:T(8,128)(2,1)}, bf16[6,768,256]{2,1,0:T(8,128)(2,1)}, bf16[6,768,256]{1,2,0:T(8,128)(2,1)}, bf16[6,768,4,64]{...) while((s32[]{:T(128)}, bf16[6,768,256]{1,2,0:T(8,128)(2,1)}, ...), condition=%wide.region_19.20_spmd, body=%wide.region_17.19_spmd.sunk | while | flops 1548886272 | bytes 131022544 | solution.py:112
  882.3 7.9 subtract_exponential_fusion.3
  896.3 14.4 %fusion.169 = bf16[4,64,768]{2,1,0:T(8,128)(2,1)S(1)} fusion(f32[4,768,768]{1,2,0:T(8,128)} %subtract_exponential_fusion.3, f32[4,768,768]{1,2,0:T(8,128)} %fusion.167, f32[768]{0:T(1024)S(1)} %broadcast_multiply_fusion.4, bf16[6,768,4,64]{1,3,2,0:T(8,128)(2,1)} %get-tuple-element.528, s32[]{:T(128)} %get-tuple-element.508), kind=kOutput, calls=%fused_computation.34.clone.1 | convolution fusion | flops 313986816 | bytes 38538752 | tf_op jit(solution)/shard_map/while/body/eval_jaxpr/hqk,qhd->khd/dot_general | solution.py:103
  911.7 15.3 %fusion.168 = bf16[4,64,768]{2,1,0:T(8,128)(2,1)} fusion(f32[4,768,768]{1,2,0:T(8,128)} %subtract_exponential_fusion.3, f32[4,768,768]{1,2,0:T(8,128)} %fusion.167, f32[768]{0:T(1024)S(1)} %broadcast_multiply_fusion.4, bf16[6,768,4,64]{1,3,2,0:T(8,128)(2,1)} %get-tuple-element.525, s32[]{:T(128)} %get-tuple-element.508), kind=kOutput, calls=%fused_computation.33.clone.1 | convolution fusion | flops 313986816 | bytes 38538752 | tf_op jit(solution)/shard_map/while/body/eval_jaxpr/hqk,khd->qhd/dot_general | solution.py:102
  951.5 14.3 %fusion.169 = bf16[4,64,768]{2,1,0:T(8,128)(2,1)S(1)} fusion(f32[4,768,768]{1,2,0:T(8,128)} %subtract_exponential_fusion.3, f32[4,768,768]{1,2,0:T(8,128)} %fusion.167, f32[768]{0:T(1024)S(1)} %broadcast_multiply_fusion.4, bf16[6,768,4,64]{1,3,2,0:T(8,128)(2,1)} %get-tuple-element.528, s32[]{:T(128)} %get-tuple-element.508), kind=kOutput, calls=%fused_computation.34.clone.1 | convolution fusion | flops 313986816 | bytes 38538752 | tf_op jit(solution)/shard_map/while/body/eval_jaxpr/hqk,qhd->khd/dot_general | solution.py:103
  966.7 15.3 %fusion.168 = bf16[4,64,768]{2,1,0:T(8,128)(2,1)} fusion(f32[4,768,768]{1,2,0:T(8,128)} %subtract_exponential_fusion.3, f32[4,768,768]{1,2,0:T(8,128)} %fusion.167, f32[768]{0:T(1024)S(1)} %broadcast_multiply_fusion.4, bf16[6,768,4,64]{1,3,2,0:T(8,128)(2,1)} %get-tuple-element.525, s32[]{:T(128)} %get-tuple-element.508), kind=kOutput, calls=%fused_computation.33.clone.1 | convolution fusion | flops 313986816 | bytes 38538752 | tf_op jit(solution)/shard_map/while/body/eval_jaxpr/hqk,khd->qhd/dot_general | solution.py:102
  1006.5 14.3 %fusion.169 = bf16[4,64,768]{2,1,0:T(8,128)(2,1)S(1)} fusion(f32[4,768,768]{1,2,0:T(8,128)} %subtract_exponential_fusion.3, f32[4,768,768]{1,2,0:T(8,128)} %fusion.167, f32[768]{0:T(1024)S(1)} %broadcast_multiply_fusion.4, bf16[6,768,4,64]{1,3,2,0:T(8,128)(2,1)} %get-tuple-element.528, s32[]{:T(128)} %get-tuple-element.508), kind=kOutput, calls=%fused_computation.34.clone.1 | convolution fusion | flops 313986816 | bytes 38538752 | tf_op jit(solution)/shard_map/while/body/eval_jaxpr/hqk,qhd->khd/dot_general | solution.py:103
  1021.8 15.3 %fusion.168 = bf16[4,64,768]{2,1,0:T(8,128)(2,1)} fusion(f32[4,768,768]{1,2,0:T(8,128)} %subtract_exponential_fusion.3, f32[4,768,768]{1,2,0:T(8,128)} %fusion.167, f32[768]{0:T(1024)S(1)} %broadcast_multiply_fusion.4, bf16[6,768,4,64]{1,3,2,0:T(8,128)(2,1)} %get-tuple-element.525, s32[]{:T(128)} %get-tuple-element.508), kind=kOutput, calls=%fused_computation.33.clone.1 | convolution fusion | flops 313986816 | bytes 38538752 | tf_op jit(solution)/shard_map/while/body/eval_jaxpr/hqk,khd->qhd/dot_general | solution.py:102
  1061.6 14.4 %fusion.169 = bf16[4,64,768]{2,1,0:T(8,128)(2,1)S(1)} fusion(f32[4,768,768]{1,2,0:T(8,128)} %subtract_exponential_fusion.3, f32[4,768,768]{1,2,0:T(8,128)} %fusion.167, f32[768]{0:T(1024)S(1)} %broadcast_multiply_fusion.4, bf16[6,768,4,64]{1,3,2,0:T(8,128)(2,1)} %get-tuple-element.528, s32[]{:T(128)} %get-tuple-element.508), kind=kOutput, calls=%fused_computation.34.clone.1 | convolution fusion | flops 313986816 | bytes 38538752 | tf_op jit(solution)/shard_map/while/body/eval_jaxpr/hqk,qhd->khd/dot_general | solution.py:103
  1076.9 15.3 %fusion.168 = bf16[4,64,768]{2,1,0:T(8,128)(2,1)} fusion(f32[4,768,768]{1,2,0:T(8,128)} %subtract_exponential_fusion.3, f32[4,768,768]{1,2,0:T(8,128)} %fusion.167, f32[768]{0:T(1024)S(1)} %broadcast_multiply_fusion.4, bf16[6,768,4,64]{1,3,2,0:T(8,128)(2,1)} %get-tuple-element.525, s32[]{:T(128)} %get-tuple-element.508), kind=kOutput, calls=%fused_computation.33.clone.1 | convolution fusion | flops 313986816 | bytes 38538752 | tf_op jit(solution)/shard_map/while/body/eval_jaxpr/hqk,khd->qhd/dot_general | solution.py:102
  1102.7 7.9 subtract_exponential_fusion.3
  1116.8 14.4 %fusion.169 = bf16[4,64,768]{2,1,0:T(8,128)(2,1)S(1)} fusion(f32[4,768,768]{1,2,0:T(8,128)} %subtract_exponential_fusion.3, f32[4,768,768]{1,2,0:T(8,128)} %fusion.167, f32[768]{0:T(1024)S(1)} %broadcast_multiply_fusion.4, bf16[6,768,4,64]{1,3,2,0:T(8,128)(2,1)} %get-tuple-element.528, s32[]{:T(128)} %get-tuple-element.508), kind=kOutput, calls=%fused_computation.34.clone.1 | convolution fusion | flops 313986816 | bytes 38538752 | tf_op jit(solution)/shard_map/while/body/eval_jaxpr/hqk,qhd->khd/dot_general | solution.py:103
  1132.1 15.3 %fusion.168 = bf16[4,64,768]{2,1,0:T(8,128)(2,1)} fusion(f32[4,768,768]{1,2,0:T(8,128)} %subtract_exponential_fusion.3, f32[4,768,768]{1,2,0:T(8,128)} %fusion.167, f32[768]{0:T(1024)S(1)} %broadcast_multiply_fusion.4, bf16[6,768,4,64]{1,3,2,0:T(8,128)(2,1)} %get-tuple-element.525, s32[]{:T(128)} %get-tuple-element.508), kind=kOutput, calls=%fused_computation.33.clone.1 | convolution fusion | flops 313986816 | bytes 38538752 | tf_op jit(solution)/shard_map/while/body/eval_jaxpr/hqk,khd->qhd/dot_general | solution.py:102
  1171.9 14.3 %fusion.169 = bf16[4,64,768]{2,1,0:T(8,128)(2,1)S(1)} fusion(f32[4,768,768]{1,2,0:T(8,128)} %subtract_exponential_fusion.3, f32[4,768,768]{1,2,0:T(8,128)} %fusion.167, f32[768]{0:T(1024)S(1)} %broadcast_multiply_fusion.4, bf16[6,768,4,64]{1,3,2,0:T(8,128)(2,1)} %get-tuple-element.528, s32[]{:T(128)} %get-tuple-element.508), kind=kOutput, calls=%fused_computation.34.clone.1 | convolution fusion | flops 313986816 | bytes 38538752 | tf_op jit(solution)/shard_map/while/body/eval_jaxpr/hqk,qhd->khd/dot_general | solution.py:103
  1187.1 15.4 %fusion.168 = bf16[4,64,768]{2,1,0:T(8,128)(2,1)} fusion(f32[4,768,768]{1,2,0:T(8,128)} %subtract_exponential_fusion.3, f32[4,768,768]{1,2,0:T(8,128)} %fusion.167, f32[768]{0:T(1024)S(1)} %broadcast_multiply_fusion.4, bf16[6,768,4,64]{1,3,2,0:T(8,128)(2,1)} %get-tuple-element.525, s32[]{:T(128)} %get-tuple-element.508), kind=kOutput, calls=%fused_computation.33.clone.1 | convolution fusion | flops 313986816 | bytes 38538752 | tf_op jit(solution)/shard_map/while/body/eval_jaxpr/hqk,khd->qhd/dot_general | solution.py:102
  1239.3 39.9 %all-reduce = (f32[512]{0:T(512)}, f32[512]{0:T(512)}, f32[512]{0:T(512)}, f32[512]{0:T(512)}, f32[512]{0:T(512)}, /*index=5*/f32[512]{0:T(512)}) all-reduce(f32[512]{0:T(512)S(1)} %get-tuple-element.318, f32[512]{0:T(512)S(1)} %get-tuple-element.236, ...), channel_id=1, replica_groups=mesh['dp'=16,'tensor'=2] {'dp','tensor'}, use_global_device_ids=true, to_apply=%region_27.28 | all-reduce | flops 3072 | bytes 24576 | tf_op jit(solution)/shard_map/psum | solution.py:224
  1281.7 32.7 %all-reduce.1 = (bf16[2,256]{1,0:T(2,128)(2,1)S(1)}, bf16[1024]{0:T(1024)(128)(2,1)S(1)}) all-reduce(bf16[2,256]{1,0:T(2,128)(2,1)S(1)} %pad_maximum_fusion.7, bf16[1024]{0:T(1024)(128)(2,1)S(1)} %copy-done.35), channel_id=1, replica_groups=mesh['dp'=16,'tensor'=2] {'dp'}, use_global_device_ids=true, to_apply=%region_24.25 | all-reduce | flops 1536 | bytes 6144 | tf_op jit(solution)/shard_map/psum | solution.py:216
  1315.6 19.9 %all-reduce.5.cloned.1.call-done = (bf16[3,512,256]{1,2,0:T(8,128)(2,1)}, bf16[256,512]{1,0:T(8,128)(2,1)}, bf16[512,1024]{1,0:T(8,128)(2,1)}, bf16[1024,512]{1,0:T(8,128)(2,1)}) async-done(((bf16[3,512,256]{1,2,0:T(8,128)(2,1)}, bf16[256,512]{1,0:T(8,128)(2,1)}, bf16[512,1024]{1,0:T(8,128)(2,1)}, bf16[1024,512]{1,0:T(8,128)(2,1)}), (bf16[3,512,256]{1,2,0:T(8,128)(2,1)}, bf16[256,512]{1,0:T(8,128)(2,1)}, ...) | async-done | bytes 3145744 | tf_op jit(solution)/shard_map/psum | solution.py:215
  1343.5 53.7 %reduce-scatter.11.cloned.1.call-done = bf16[2304,512]{1,0:T(8,128)(2,1)} async-done(((bf16[4608,512]{1,0:T(8,128)(2,1)}), bf16[2304,512]{1,0:T(8,128)(2,1)}) %reduce-scatter.11.cloned.1.call-update) | async-done | bytes 2359312 | tf_op jit(solution)/shard_map/reduce_scatter | solution.py:208
  (327 shorter events, 395.2 us)
Async XLA Ops:
  7.2 386.4 %copy-start = (bf16[512,1024]{1,0:T(8,128)(2,1)S(1)}, bf16[512,1024]{1,0:T(8,128)(2,1)}, u32[]{:S(2)}) copy-start(bf16[512,1024]{1,0:T(8,128)(2,1)} %param.33) | copy-start | bytes 3145732
  7.2 67.8 %all-gather.5.cloned.1.call-start = ((), (), s32[]{:S(2)}) async-start(), calls=%async_computation.4 | async-start | bytes 7077888 | tf_op jit(solution)/shard_map/all_gather | solution.py:156
  7.9 314.6 %reduce-scatter.5.cloned.1.call-start = ((), (), s32[]{:S(2)}) async-start(), calls=%async_computation.5 | async-start | bytes 14155776 | tf_op jit(solution)/shard_map/reduce_scatter | solution.py:159
  122.4 82.7 %copy-start.19 = (bf16[256,512]{1,0:T(8,128)(2,1)S(1)}, bf16[256,512]{1,0:T(8,128)(2,1)}, u32[]{:S(2)}) copy-start(bf16[256,512]{1,0:T(8,128)(2,1)} %param.29) | copy-start | bytes 786436
  211.8 110.8 %copy-start.9 = (bf16[2304,512]{1,0:T(8,128)(2,1)S(1)}, bf16[2304,512]{1,0:T(8,128)(2,1)}, u32[]{:S(2)}) copy-start(bf16[2304,512]{1,0:T(8,128)(2,1)} %param.22) | copy-start | bytes 7077892
  211.8 110.7 %copy-start.37 = (f32[512]{0:T(512)S(1)}, f32[512]{0:T(512)}, u32[]{:S(2)}) copy-start(f32[512]{0:T(512)} %param.30) | copy-start | bytes 6148
  211.8 181.7 %all-gather.7.cloned.1.call-start = ((), (), s32[]{:S(2)}) async-start(), calls=%async_computation.6 | async-start | bytes 7077888 | tf_op jit(solution)/shard_map/all_gather | solution.py:165
  328.4 65.2 %copy-start.41 = (f32[1024]{0:T(1024)S(1)}, f32[1024]{0:T(1024)}, u32[]{:S(2)}) copy-start(f32[1024]{0:T(1024)} %param.34) | copy-start | bytes 12292
  330.8 113.9 %copy-start.40 = (bf16[1024,512]{1,0:T(8,128)(2,1)S(1)}, bf16[1024,512]{1,0:T(8,128)(2,1)}, u32[]{:S(2)}) copy-start(bf16[1024,512]{1,0:T(8,128)(2,1)} %param.35) | copy-start | bytes 3145732
  330.8 232.2 %reduce-scatter.7.cloned.1.call-start = ((), (), s32[]{:S(2)}) async-start(), calls=%async_computation.7 | async-start | bytes 14155776 | tf_op jit(solution)/shard_map/reduce_scatter | solution.py:168
  452.2 110.8 %copy-start.16 = (f32[2304]{0:T(1024)S(1)}, f32[2304]{0:T(1024)}, u32[]{:S(2)}) copy-start(f32[2304]{0:T(1024)} %copy-done.15) | copy-start | bytes 27652
  452.2 110.8 %copy-start.18 = (f32[2304]{0:T(1024)S(1)}, f32[2304]{0:T(1024)}, u32[]{:S(2)}) copy-start(f32[2304]{0:T(1024)} %copy-done.17) | copy-start | bytes 27652
  452.2 110.8 %copy-start.27 = (f32[512]{0:T(512)S(1)}, f32[512]{0:T(512)}, u32[]{:S(2)}) copy-start(f32[512]{0:T(512)} %param.31) | copy-start | bytes 6148
  452.2 110.8 %copy-start.32 = (f32[512]{0:T(512)S(1)}, f32[512]{0:T(512)}, u32[]{:S(2)}) copy-start(f32[512]{0:T(512)} %param.32) | copy-start | bytes 6148
  452.2 110.8 %copy-start.34 = (f32[512]{0:T(512)S(1)}, f32[512]{0:T(512)}, u32[]{:S(2)}) copy-start(f32[512]{0:T(512)} %param.36) | copy-start | bytes 6148
  452.2 191.0 %all-gather.9.cloned.1.call-start = ((), (), s32[]{:S(2)}) async-start(), calls=%async_computation.8 | async-start | bytes 7077888 | tf_op jit(solution)/shard_map/all_gather | solution.py:175
  580.4 205.7 %reduce-scatter.9.cloned.1.call-start = ((), (), s32[]{:S(2)}) async-start(), calls=%async_computation.9 | async-start | bytes 14155776 | tf_op jit(solution)/shard_map/reduce_scatter | solution.py:184
  675.4 117.0 %copy-start.25 = (f32[2304]{0:T(1024)S(1)}, f32[2304]{0:T(1024)}, u32[]{:S(2)}) copy-start(f32[2304]{0:T(1024)} %copy-done.24) | copy-start | bytes 27652
  675.4 188.3 %all-gather.11.cloned.1.call-start = ((), (), s32[]{:S(2)}) async-start(), calls=%async_computation.10 | async-start | bytes 7077888 | tf_op jit(solution)/shard_map/all_gather | solution.py:189
  799.0 12.0 slice-start
  800.9 534.7 %all-reduce.5.cloned.1.call-start = ((), (), s32[]{:S(2)}) async-start(), calls=%async_computation.12 | async-start | bytes 6291456 | tf_op jit(solution)/shard_map/psum | solution.py:215
  879.6 10.7 copy-start.4
  911.7 17.1 %copy-start.5 = (bf16[6,768,4,64]{1,3,2,0:T(8,128)(2,1)S(1)}, bf16[6,768,4,64]{1,3,2,0:T(8,128)(2,1)}, u32[]{:S(2)}) copy-start(bf16[6,768,4,64]{1,3,2,0:T(8,128)(2,1)} %copy-done.4) | copy-start | bytes 7077892 | tf_op jit(solution)/shard_map/while
  966.7 17.1 %copy-start.5 = (bf16[6,768,4,64]{1,3,2,0:T(8,128)(2,1)S(1)}, bf16[6,768,4,64]{1,3,2,0:T(8,128)(2,1)}, u32[]{:S(2)}) copy-start(bf16[6,768,4,64]{1,3,2,0:T(8,128)(2,1)} %copy-done.4) | copy-start | bytes 7077892 | tf_op jit(solution)/shard_map/while
  1021.8 17.1 %copy-start.5 = (bf16[6,768,4,64]{1,3,2,0:T(8,128)(2,1)S(1)}, bf16[6,768,4,64]{1,3,2,0:T(8,128)(2,1)}, u32[]{:S(2)}) copy-start(bf16[6,768,4,64]{1,3,2,0:T(8,128)(2,1)} %copy-done.4) | copy-start | bytes 7077892 | tf_op jit(solution)/shard_map/while
  1076.9 17.1 %copy-start.5 = (bf16[6,768,4,64]{1,3,2,0:T(8,128)(2,1)S(1)}, bf16[6,768,4,64]{1,3,2,0:T(8,128)(2,1)}, u32[]{:S(2)}) copy-start(bf16[6,768,4,64]{1,3,2,0:T(8,128)(2,1)} %copy-done.4) | copy-start | bytes 7077892 | tf_op jit(solution)/shard_map/while
  1100.0 10.6 copy-start.4
  1132.1 17.1 %copy-start.5 = (bf16[6,768,4,64]{1,3,2,0:T(8,128)(2,1)S(1)}, bf16[6,768,4,64]{1,3,2,0:T(8,128)(2,1)}, u32[]{:S(2)}) copy-start(bf16[6,768,4,64]{1,3,2,0:T(8,128)(2,1)} %copy-done.4) | copy-start | bytes 7077892 | tf_op jit(solution)/shard_map/while
  1187.1 17.2 %copy-start.5 = (bf16[6,768,4,64]{1,3,2,0:T(8,128)(2,1)S(1)}, bf16[6,768,4,64]{1,3,2,0:T(8,128)(2,1)}, u32[]{:S(2)}) copy-start(bf16[6,768,4,64]{1,3,2,0:T(8,128)(2,1)} %copy-done.4) | copy-start | bytes 7077892 | tf_op jit(solution)/shard_map/while
  1231.1 166.1 %reduce-scatter.11.cloned.1.call-start = ((), (), s32[]{:S(2)}) async-start(), calls=%async_computation.11 | async-start | bytes 7077888 | tf_op jit(solution)/shard_map/reduce_scatter | solution.py:208
  1238.6 40.6 %copy-start.8 = (bf16[6,768,256]{1,2,0:T(8,128)(2,1)S(1)}, bf16[6,768,256]{1,2,0:T(8,128)(2,1)}, u32[]{:S(2)}) copy-start(bf16[6,768,256]{1,2,0:T(8,128)(2,1)} %get-tuple-element.128) | copy-start | bytes 7077892
  1238.6 43.1 %copy-start.35 = (bf16[1024]{0:T(1024)(128)(2,1)S(1)}, bf16[1024]{0:T(1024)(128)(2,1)}, u32[]{:S(2)}) copy-start(bf16[1024]{0:T(1024)(128)(2,1)} %get-tuple-element.296) | copy-start | bytes 6148
  (32 other events, 158.8 us)
Sparse Core Ops, SparseCore 0:
  9.6 65.3 all-gather.4
  212.0 110.5 reduce-scatter.4
  330.9 62.6 all-gather.6
  452.4 110.5 reduce-scatter.6
  580.5 62.6 all-gather.8
  675.5 110.5 reduce-scatter.8
  801.0 62.6 all-gather.10
  1231.3 104.2 all-reduce.4
  1338.4 58.7 reduce-scatter.10
where the time goes:
time: 1420 us; the launch traced here: 1410 us
  waiting for transfers between devices  635 us (45%)
  matrix products  497 us (35%)
  local copies, waits for them, and re-layouts  112 us (8%)
  other arithmetic  76.9 us (5%)
  blocking collectives  72.6 us (5%)
  between operations  14.8 us (1%)
    reduce_scatter x1, waiting for transfers between devices, on_device(): lax.psum_scatter(row_term(attended, merge_weight, 'tc,cd->td'), 'tensor',...  111 us
    reduce_scatter x1, waiting for transfers between devices, on_device(): lax.psum_scatter(row_term(active, reduce_weight, 'tf,fd->td'), 'tensor',...  111 us
    reduce_scatter x1, waiting for transfers between devices, on_device(): lax.psum_scatter(row_term(grad_preact, expand_weight, 'tf,df->td'), 'tens...  111 us
    dot_general x6, matrix products, one_block(): jnp.einsum('hqk,khd->qhd', lowered, block_k, preferred_element_type=jnp.f...  92 us
    dot_general x6, matrix products, one_block(): jnp.einsum('hqk,qhd->khd', lowered, block_q, preferred_element_type=jnp.f...  86 us
    dot_general x12, matrix products, block_scores(): jnp.einsum('qhd,khd->hqk', block_q, block_k, preferred_element_type=jnp.f...  72.3 us
    all_gather x1, waiting for transfers between devices, on_device(): lax.all_gather(grad_second.astype(jnp.bfloat16), 'tensor', axis=0, tiled=...  62.8 us
    all_gather x1, waiting for transfers between devices, on_device(): feed_all = lax.all_gather(normed_low, 'tensor', axis=0, tiled=True)  62.8 us
  transfers between devices with their start and end apart: 9, of which 9 were waited for; matrix products, arithmetic and copies ran while one was open for 3% of the time, Pallas kernels for 0%

commit v1 on v0

--- a/solution.py
+++ b/solution.py
@@ -1,12 +1,19 @@
+import functools
 import jax
 import jax.numpy as jnp
 from jax import lax
+from jax.experimental import pallas as pl
+from jax.experimental.pallas import tpu as pltpu
 from jax.sharding import PartitionSpec as P
 
 HEAD = 64
 SHORT = 96
 LONG = 384
 TABLE = 64
+PAIR = 2 * HEAD
+LOG2E = 1.4426950408889634
+F32 = jnp.float32
+BF16 = jnp.bfloat16
 
 
 def layer_norm(values, gain, shift):
@@ -132,7 +139,7 @@
     return (grad_reduce_weight, grad_preact, grad_expand_bias, grad_expand_weight)
 
 
-def on_device(
+def split_layer(
     inputs,
     pack_long,
     item_table,
@@ -243,6 +250,611 @@
     )
 
 
+def mm(a, b):
+    return lax.dot_general(a, b, (((1,), (0,)), ((), ())), preferred_element_type=F32)
+
+
+def mm_nt(a, b):
+    return lax.dot_general(a, b, (((1,), (1,)), ((), ())), preferred_element_type=F32)
+
+
+def mm_tn(a, b):
+    return lax.dot_general(a, b, (((0,), (0,)), ((), ())), preferred_element_type=F32)
+
+
+def col_sum(v):
+    return jnp.sum(v, axis=0, keepdims=True)
+
+
+def row_mean(v):
+    return jnp.mean(v, axis=1, keepdims=True)
+
+
+def pack_rows(pack, long_ref, item_ref):
+    per = LONG // SHORT
+    longer = long_ref[pack] == 1
+    rows = [jnp.where(longer, item_ref[pack * per], item_ref[pack * per + k]) for k in range(per)]
+    return longer, rows
+
+
+def pack_tau(rows, tau_ref):
+    slot = lax.broadcasted_iota(jnp.int32, (LONG, 1), 0) // SHORT
+    tau = jnp.full((LONG, 1), tau_ref[rows[0]], F32)
+    for k in range(1, LONG // SHORT):
+        tau = jnp.where(slot == k, tau_ref[rows[k]], tau)
+    return tau
+
+
+def pack_bias(longer, rows, delta_ref):
+    slot_r = lax.broadcasted_iota(jnp.int32, (LONG, 1), 0) // SHORT
+    slot_c = lax.broadcasted_iota(jnp.int32, (1, LONG), 1) // SHORT
+    shift = delta_ref[pl.ds(rows[0], 1), :]
+    for k in range(1, LONG // SHORT):
+        piece = jnp.broadcast_to(delta_ref[pl.ds(rows[k], 1), :], (8, LONG))
+        piece = pltpu.roll(piece, SHORT * k, 1)[0:1]
+        shift = jnp.where(jnp.logical_and(jnp.logical_not(longer), slot_c == k), piece, shift)
+    mask = jnp.logical_or(longer, slot_r == slot_c)
+    return jnp.where(mask, shift * (HEAD**-0.5 * LOG2E), -1e30)
+
+
+def forward_kernel(
+    place, long_ref, item_ref, tau_ref, delta_ref, x_ref, wa_ref, wb_ref, b_ref,
+    q_ref, k_ref, v_ref, o_ref, r_ref, p_ref, w_ref, bias_ref,
+):
+    step = pl.program_id(0)
+
+    @pl.when(step == 0)
+    def _():
+        w_ref[:, :, :PAIR] = wa_ref[...]
+        w_ref[:, :, PAIR:] = wb_ref[...]
+
+    longer, rows = pack_rows(step + place[1], long_ref, item_ref)
+    bias_ref[...] = pack_bias(longer, rows, delta_ref)
+    tau = pack_tau(rows, tau_ref) * (HEAD**-0.5 * LOG2E)
+    x = x_ref[...]
+    q = (mm(x, w_ref[0]) + b_ref[0:1]).astype(BF16)
+    k = mm(x, w_ref[1]).astype(BF16)
+    v = (mm(x, w_ref[2]) + b_ref[1:2]).astype(BF16)
+    q_ref[...] = q
+    k_ref[...] = k
+    v_ref[...] = v
+    scaled = (q.astype(F32) * tau).astype(BF16)
+    vf = v.astype(F32)
+    first = lax.broadcasted_iota(jnp.int32, (1, PAIR), 1) < HEAD
+    heads = q.shape[1] // HEAD
+
+    def score(h):
+        at = slice(h * HEAD, (h + 1) * HEAD)
+        return mm_nt(scaled[:, at], k[:, at])
+
+    def soften(s):
+        s = s + bias_ref[...]
+        return jnp.exp2(s - jnp.max(s, axis=1, keepdims=True)).astype(BF16)
+
+    mixed = []
+
+    def mix(h, w):
+        p_ref[0, h] = w
+        at = slice(h // 2 * PAIR, (h // 2 + 1) * PAIR)
+        own = first if h % 2 == 0 else jnp.logical_not(first)
+        mixed.append(mm(w, jnp.where(own, vf[:, at], 1.0).astype(BF16)))
+        if h % 2 == 1:
+            a, b = mixed[-2:]
+            r = 1.0 / pltpu.roll(jnp.where(first, b, a), HEAD, 1)
+            r_ref[:, at] = r
+            o_ref[:, at] = (jnp.where(first, a, b) * r).astype(BF16)
+
+    s = score(0)
+    held = None
+    for h in range(heads):
+        later = score(h + 1) if h + 1 < heads else None
+        w = soften(s)
+        if held is not None:
+            mix(h - 1, held)
+        held, s = w, later
+    mix(heads - 1, held)
+
+
+def whole(shape):
+    return pl.BlockSpec(shape, lambda *_: (0,) * len(shape), pipeline_mode=pl.Buffered(1))
+
+
+def smem():
+    return pl.BlockSpec(memory_space=pltpu.SMEM)
+
+
+def kernel_params():
+    return pltpu.CompilerParams(vmem_limit_bytes=60 * 2**20)
+
+
+def cost(us):
+    return pl.CostEstimate(flops=int(us * 1.0e9), bytes_accessed=0, transcendentals=0)
+
+
+def attend(place, long_, item, tau, delta, x, wa, wb, bias, own):
+    n, d = x.shape
+    packs = n // LONG
+    cols = 2 * PAIR
+    row = lambda c: pl.BlockSpec((LONG, c), lambda i, *_: (i, 0))
+    pick = (lambda h: lambda i, place, *_: (0, 0, place[0] ^ h)) if own else (lambda h: lambda *_: (0, 0, 0))
+    out = jax.ShapeDtypeStruct((n, cols), BF16)
+    heads = cols // HEAD
+    return pl.pallas_call(
+        forward_kernel,
+        grid_spec=pltpu.PrefetchScalarGridSpec(
+            num_scalar_prefetch=3,
+            grid=(packs,),
+            in_specs=[smem(), whole(delta.shape), row(d)]
+            + [
+                pl.BlockSpec((3, d, PAIR), pick(h), pipeline_mode=pl.Buffered(1)) for h in (0, 1)
+            ]
+            + [whole(bias.shape)],
+            out_specs=[row(cols)] * 5
+            + [pl.BlockSpec((1, heads, LONG, LONG), lambda i, *_: (i, 0, 0, 0))],
+            scratch_shapes=[pltpu.VMEM((3, d, cols), BF16), pltpu.VMEM((LONG, LONG), F32)],
+        ),
+        out_shape=[out] * 4
+        + [
+            jax.ShapeDtypeStruct((n, cols), F32),
+            jax.ShapeDtypeStruct((packs, heads, LONG, LONG), BF16),
+        ],
+        compiler_params=kernel_params(),
+        cost_estimate=cost(11),
+        name="attend_own" if own else "attend_other",
+    )(place, long_, item, tau, delta, x, wa, wb, bias)
+
+
+def gelu_parts(u):
+    z = jnp.abs(u)
+    t = 1.0 / (1.0 + (0.3275911 * 0.7071067811865476) * z)
+    e = jnp.exp2(u * u * (-0.5 * LOG2E))
+    poly = 0.5 * -1.453152027 + t * (0.5 * 1.061405429)
+    poly = 0.5 * -0.284496736 + t * (0.5 * 1.421413741 + t * poly)
+    tail = t * (0.5 * 0.254829592 + t * poly) * e
+    return jnp.where(u >= 0, 1.0 - tail, tail), e
+
+
+def feed_kernel(
+    place, o0_ref, o1_ref, x_ref, gy_ref, mk_ref, ms_ref, ek_ref, es_ref, rk_ref, rs_ref,
+    near_ref, far_ref, be_ref, vec_ref,
+    out_ref, dh1_ref, do_ref, grad_ref, sum_ref, sbe_ref,
+    wm_ref, act_ref, du_ref, gp_ref, n1_ref, dh2_ref, dh1b_ref, o_ref, *, tiles, tile,
+):
+    step = pl.program_id(0)
+    d = x_ref.shape[1]
+    hid = ek_ref.shape[1]
+    mrows = mk_ref.shape[0]
+    half = 2 * mrows
+    expand = (ek_ref, es_ref, near_ref.at[0:d], far_ref.at[0:d])
+    reduce_ = (rk_ref, rs_ref, near_ref.at[d:d + hid], far_ref.at[d:d + hid])
+
+    @pl.when(step == 0)
+    def _():
+        wm_ref[0:mrows] = mk_ref[...]
+        wm_ref[mrows:half] = ms_ref[...]
+        wm_ref[half:half + mrows] = near_ref[d + hid:]
+        wm_ref[half + mrows:] = far_ref[d + hid:]
+
+    @pl.when(step < tiles)
+    def _():
+        here = pl.ds(pl.multiple_of(step * tile, tile), tile)
+        bm, g1, b1, br, g2, b2 = [vec_ref[k:k + 1] for k in range(6)]
+        o0, o1 = o0_ref[...], o1_ref[...]
+        o_ref[here, :half] = o0
+        o_ref[here, half:] = o1
+        h1 = x_ref[...].astype(F32) + (mm(o0, wm_ref[:half]) + mm(o1, wm_ref[half:]) + bm)
+        c = h1 - row_mean(h1)
+        rs = lax.rsqrt(row_mean(c * c) + 1e-05)
+        xh = c * rs
+        n1 = xh * g1 + b1
+        low = n1.astype(BF16)
+        n1_ref[here] = low
+        u = mm(low, expand[0][...])
+        fed = n1 + br
+        for k in range(4):
+            later = mm(low, expand[k + 1][...]) if k < 3 else None
+            at = slice(k * hid, (k + 1) * hid)
+            u = u + be_ref[0:1, at]
+            phi, e = gelu_parts(u)
+            act = (u * phi).astype(BF16)
+            act_ref[here, at] = act
+            gp_ref[:, at] = (phi + u * (e * 0.3989422804014327)).astype(BF16)
+            fed = fed + mm(act, reduce_[k][...])
+            u = later
+        c2 = fed - row_mean(fed)
+        rs2 = lax.rsqrt(row_mean(c2 * c2) + 1e-05)
+        xh2 = c2 * rs2
+        out_ref[...] = xh2 * g2 + b2
+        gy = gy_ref[...].astype(F32)
+        gg = gy * g2
+        dh2 = rs2 * ((gg - row_mean(gg)) - xh2 * row_mean(gg * xh2))
+        dh2b = dh2.astype(BF16)
+        dh2_ref[here] = dh2b
+        dn = dh2
+        sbe = []
+        da = mm_nt(dh2b, reduce_[0][...])
+        for k in range(4):
+            later = mm_nt(dh2b, reduce_[k + 1][...]) if k < 3 else None
+            at = slice(k * hid, (k + 1) * hid)
+            du = (da * gp_ref[:, at].astype(F32)).astype(BF16)
+            du_ref[here, at] = du
+            sbe.append(col_sum(du.astype(F32)))
+            dn = dn + mm_nt(du, expand[k][...])
+            da = later
+        gg1 = dn * g1
+        dh1 = rs * ((gg1 - row_mean(gg1)) - xh * row_mean(gg1 * xh))
+        dh1_ref[...] = dh1
+        dh1b = dh1.astype(BF16)
+        dh1b_ref[here] = dh1b
+        do_ref[...] = mm_nt(dh1b, wm_ref[...]).astype(BF16)
+        sums = [col_sum(dh1), col_sum(dn * xh), col_sum(dn), col_sum(dh2), col_sum(gy * xh2), col_sum(gy)]
+        sums = jnp.concatenate(sums + [jnp.zeros((2, d), F32)], axis=0)
+        sbe = jnp.broadcast_to(jnp.concatenate(sbe, axis=1), sbe_ref.shape)
+
+        @pl.when(step == 0)
+        def _():
+            sum_ref[...] = sums
+            sbe_ref[...] = sbe
+
+        @pl.when(step > 0)
+        def _():
+            sum_ref[...] += sums
+            sbe_ref[...] += sbe
+
+    for quarter in range(4):
+
+        @pl.when(step == tiles + quarter)
+        def _(quarter=quarter):
+            at = slice(quarter * hid, (quarter + 1) * hid)
+            om = slice(quarter * mrows, (quarter + 1) * mrows)
+            grad_ref[0, 0:hid] = mm_tn(act_ref[:, at], dh2_ref[...]).astype(BF16)
+            grad_ref[0, hid:hid + d] = mm_tn(n1_ref[...], du_ref[:, at]).astype(BF16)
+            grad_ref[0, hid + d:] = mm_tn(o_ref[:, om], dh1b_ref[...]).astype(BF16)
+
+
+def feed(place, o0, o1, x, gy, merge, expand, reduce_, near, far, be, vec):
+    n, d = x.shape
+    tile = LONG
+    tiles = n // tile
+    mrows, hid = merge.shape[0] // 2, expand.shape[1] // 2
+    full_hid = 4 * hid
+    at = lambda i: jnp.minimum(i, tiles - 1)
+    row = lambda c: pl.BlockSpec((tile, c), lambda i, *_: (at(i), 0))
+    once = pl.Buffered(1)
+    by_row = lambda shape, h: pl.BlockSpec(shape, lambda i, place: (place[0] ^ h, 0), pipeline_mode=once)
+    by_col = lambda shape, h: pl.BlockSpec(shape, lambda i, place: (0, place[0] ^ h), pipeline_mode=once)
+    S = jax.ShapeDtypeStruct
+    grows = hid + d + mrows
+    return pl.pallas_call(
+        functools.partial(feed_kernel, tiles=tiles, tile=tile),
+        grid_spec=pltpu.PrefetchScalarGridSpec(
+            num_scalar_prefetch=1,
+            grid=(tiles + 4,),
+            in_specs=[row(o0.shape[1]), row(o1.shape[1]), row(d), row(d)]
+            + [by_row((mrows, d), h) for h in (0, 1)]
+            + [by_col((d, hid), h) for h in (0, 1)]
+            + [by_row((hid, d), h) for h in (0, 1)]
+            + [whole(near.shape), whole(far.shape), whole(be.shape), whole(vec.shape)],
+            out_specs=[row(d), row(d), row(d)]
+            + [
+                pl.BlockSpec((1, grows, d), lambda i, *_: (jnp.maximum(i - tiles, 0), 0, 0)),
+                pl.BlockSpec((8, d), lambda i, *_: (0, 0)),
+                pl.BlockSpec((8, full_hid), lambda i, *_: (0, 0)),
+            ],
+            scratch_shapes=[
+                pltpu.VMEM((4 * mrows, d), BF16),
+                pltpu.VMEM((n, full_hid), BF16),
+                pltpu.VMEM((n, full_hid), BF16),
+                pltpu.VMEM((tile, full_hid), BF16),
+                pltpu.VMEM((n, d), BF16),
+                pltpu.VMEM((n, d), BF16),
+                pltpu.VMEM((n, d), BF16),
+                pltpu.VMEM((n, 4 * mrows), BF16),
+            ],
+        ),
+        out_shape=[S((n, d), F32), S((n, d), F32), S((n, d), BF16), S((4, grows, d), BF16)]
+        + [S((8, d), F32), S((8, full_hid), F32)],
+        compiler_params=kernel_params(),
+        cost_estimate=cost(60),
+        name="feed",
+    )(place, o0, o1, x, gy, merge, merge, expand, expand, reduce_, reduce_, near, far, be, vec)
+
+
+def backward_kernel(
+    place, long_ref, item_ref, tau_ref, q_ref, k_ref, v_ref, g_ref, o_ref, r_ref, p_ref,
+    dq_ref, dk_ref, dv_ref,
+):
+    _, rows = pack_rows(pl.program_id(0) + place[1], long_ref, item_ref)
+    tau = pack_tau(rows, tau_ref) * HEAD**-0.5
+    heads = q_ref.shape[1] // HEAD
+    lane = lax.broadcasted_iota(jnp.int32, (1, PAIR), 1)
+    first = lane < HEAD
+    ready = []
+    for i in range(heads // 2):
+        at = slice(i * PAIR, (i + 1) * PAIR)
+        g = g_ref[:, at].astype(F32) * r_ref[:, at]
+        low = g.astype(BF16)
+        scaled = (g * tau).astype(BF16).astype(F32)
+        d = scaled * o_ref[:, at].astype(F32)
+        v = v_ref[:, at].astype(F32)
+        for j in range(2):
+            own = first if j == 0 else jnp.logical_not(first)
+            spare = HEAD if j == 0 else 0
+            dd = jnp.sum(jnp.where(own, d, 0.0), axis=1, keepdims=True)
+            high = dd.astype(BF16).astype(F32)
+            left = jnp.where(lane == spare, -high, jnp.where(lane == spare + 1, high - dd, 0.0))
+            left = jnp.where(own, scaled, left).astype(BF16)
+            ones = jnp.where(jnp.logical_or(lane == spare, lane == spare + 1), 1.0, 0.0)
+            right = jnp.where(own, v, ones).astype(BF16)
+            ready.append((left, right, low[:, j * HEAD:(j + 1) * HEAD]))
+
+    def score(h):
+        return mm_nt(ready[h][0], ready[h][1])
+
+    res = []
+    t = score(0)
+    for h in range(heads):
+        later = score(h + 1) if h + 1 < heads else None
+        at = slice(h * HEAD, (h + 1) * HEAD)
+        w = p_ref[0, h]
+        r = (w.astype(F32) * t).astype(BF16)
+        res.append((mm(r, k_ref[:, at]), mm_tn(q_ref[:, at], r), mm_tn(ready[h][2], w)))
+        t = later
+    for i in range(heads // 2):
+        at = slice(i * PAIR, (i + 1) * PAIR)
+        a, b = res[2 * i], res[2 * i + 1]
+        dq_ref[:, at] = jnp.concatenate([a[0], b[0]], axis=1).astype(BF16)
+        dk_ref[:, at] = jnp.concatenate([a[1], b[1]], axis=0).T.astype(BF16)
+        dv_ref[:, at] = jnp.concatenate([a[2], b[2]], axis=0).T.astype(BF16)
+
+
+def attend_back(place, long_, item, tau, q, k, v, g, o, r, p, slot):
+    n, cols = q.shape
+    packs = n // LONG
+    row = lambda c: pl.BlockSpec((LONG, c), lambda i, *_: (i, 0))
+    out = jax.ShapeDtypeStruct((n, cols), BF16)
+    return pl.pallas_call(
+        backward_kernel,
+        grid_spec=pltpu.PrefetchScalarGridSpec(
+            num_scalar_prefetch=3,
+            grid=(packs,),
+            in_specs=[smem()]
+            + [row(cols)] * 3
+            + [pl.BlockSpec((LONG, cols), lambda i, *_: (i, slot))]
+            + [row(cols)] * 2
+            + [pl.BlockSpec((1,) + p.shape[1:], lambda i, *_: (i, 0, 0, 0))],
+            out_specs=[row(cols)] * 3,
+        ),
+        out_shape=[out] * 3,
+        compiler_params=kernel_params(),
+        cost_estimate=cost(11),
+        name="attend_back%d" % slot,
+    )(place, long_, item, tau, q, k, v, g, o, r, p)
+
+
+def project_grad_kernel(x_ref, *refs):
+    d_refs, (grad_ref, sum_ref) = refs[:-2], refs[-2:]
+    depth = x_ref.shape[1]
+    for k, d_ref in enumerate(d_refs):
+        slot, j = divmod(k, 3)
+
+        @pl.when(pl.program_id(0) == k)
+        def _(slot=slot, j=j, d_ref=d_ref):
+            d = d_ref[...]
+            res = mm_tn(x_ref[...], d).astype(BF16)
+            grad_ref[slot, 0, j * depth:(j + 1) * depth] = res[:, :PAIR]
+            grad_ref[slot, 1, j * depth:(j + 1) * depth] = res[:, PAIR:]
+            if j != 1:
+                row = slot * 2 + j // 2
+                sum_ref[row:row + 1] = col_sum(d.astype(F32))
+
+
+def project_grad(x, grads):
+    n, d = x.shape
+    cols = grads[0].shape[1]
+    S = jax.ShapeDtypeStruct
+    return pl.pallas_call(
+        project_grad_kernel,
+        grid=(6,),
+        in_specs=[whole(x.shape)] + [whole(g.shape) for g in grads],
+        out_specs=[
+            pl.BlockSpec((2, 2, 3 * d, PAIR), lambda i: (0, 0, 0, 0)),
+            pl.BlockSpec((8, cols), lambda i: (0, 0)),
+        ],
+        out_shape=[S((2, 2, 3 * d, PAIR), BF16), S((8, cols), F32)],
+        compiler_params=kernel_params(),
+        cost_estimate=cost(7),
+        name="project_grad",
+    )(x, *grads)
+
+
+def input_grad_kernel(place, dh1_ref, ka_ref, sa_ref, near_ref, far_ref, *refs):
+    d_refs, (out_ref, w_ref) = refs[:-2], refs[-2:]
+
+    @pl.when(pl.program_id(0) == 0)
+    def _():
+        for j in range(3):
+            for k, ref in enumerate((ka_ref, sa_ref, near_ref, far_ref)):
+                slot, h = divmod(k, 2)
+                lo = (slot * 3 + j) * 2 * PAIR + h * PAIR
+                w_ref[:, lo:lo + PAIR] = ref[j]
+
+    d = jnp.concatenate([ref[...] for ref in d_refs], axis=1)
+    out_ref[...] = dh1_ref[...] + mm_nt(d, w_ref[...])
+
+
+def input_grad(place, dh1, weight, near, far, grads):
+    n, d = dh1.shape
+    tile = 2 * LONG if n % (2 * LONG) == 0 else LONG
+    cols = grads[0].shape[1]
+    row = lambda c: pl.BlockSpec((tile, c), lambda i, *_: (i, 0))
+    pick = lambda h: pl.BlockSpec((3, d, PAIR), lambda i, place: (0, 0, place[0] ^ h), pipeline_mode=pl.Buffered(1))
+    return pl.pallas_call(
+        input_grad_kernel,
+        grid_spec=pltpu.PrefetchScalarGridSpec(
+            num_scalar_prefetch=1,
+            grid=(n // tile,),
+            in_specs=[row(d), pick(0), pick(1), whole(near.shape), whole(far.shape)] + [row(cols)] * 6,
+            out_specs=row(d),
+            scratch_shapes=[pltpu.VMEM((d, 6 * cols), BF16)],
+        ),
+        out_shape=jax.ShapeDtypeStruct((n, d), F32),
+        compiler_params=kernel_params(),
+        cost_estimate=cost(6),
+        name="input_grad",
+    )(place, dh1, weight, weight, near, far, *grads)
+
+
+def flip(v, axis, mask):
+    size = lax.axis_size(axis)
+    return lax.ppermute(v, axis, [(i, i ^ mask) for i in range(size)])
+
+
+def add_low(*parts):
+    return functools.reduce(lambda a, b: a + b, [p.astype(F32) for p in parts]).astype(BF16)
+
+
+def sum_quarters(grad, dp_size):
+    core = lax.axis_index("dp") % 2
+    got = flip(grad[:, 1], "dp", 1)
+    far = flip(add_low(grad[1, 0], got[1]), "tensor", 1)
+    mine = add_low(grad[0, 0], got[0], far)
+    rows = mine.shape[0] // 2
+    bit = lax.axis_index("dp") // 2 % 2
+    send = lax.dynamic_slice_in_dim(mine, (1 - bit) * rows, rows, 0)
+    keep = lax.dynamic_slice_in_dim(mine, bit * rows, rows, 0)
+    total = add_low(keep, flip(send, "dp", 2))
+    mask = 4
+    while mask < dp_size:
+        total = add_low(total, flip(total, "dp", mask))
+        mask *= 2
+    other = flip(total, "dp", 2)
+    total = jnp.where(bit == 0, jnp.concatenate([total, other]), jnp.concatenate([other, total]))
+    other = flip(total, "dp", 1)
+    return jnp.where(core == 0, jnp.stack([total, other]), jnp.stack([other, total]))
+
+
+def ordered(v, core):
+    cols = v.shape[-1] // 2
+    return jnp.where(core == 0, v, jnp.concatenate([v[..., cols:], v[..., :cols]], axis=-1))
+
+
+def row_layer(
+    inputs,
+    pack_long,
+    item_table,
+    tau_table,
+    delta_table,
+    project_weight,
+    project_bias,
+    merge_weight,
+    merge_bias,
+    first_gain,
+    first_shift,
+    expand_weight,
+    expand_bias,
+    reduce_weight,
+    reduce_bias,
+    second_gain,
+    second_shift,
+    grad_output,
+    dp_size,
+):
+    n, d = inputs.shape
+    hid = expand_weight.shape[1] // 2
+    mrows = merge_weight.shape[0] // 2
+    core = lax.axis_index("dp") % 2
+    place = jnp.stack([core, lax.axis_index("tensor") * (n // LONG)]).astype(jnp.int32)
+
+    project_near = flip(lax.dynamic_slice_in_dim(project_weight, core * PAIR, PAIR, 2), "tensor", 1)
+    biases = flip(jnp.concatenate([project_bias.reshape(-1), expand_bias]), "tensor", 1)
+    rest = jnp.concatenate(
+        [
+            lax.dynamic_slice_in_dim(expand_weight, core * hid, hid, 1),
+            lax.dynamic_slice_in_dim(reduce_weight, core * hid, hid, 0),
+            lax.dynamic_slice_in_dim(merge_weight, core * mrows, mrows, 0),
+        ],
+        axis=0,
+    )
+    rest_near = flip(rest, "tensor", 1)
+    project_far = flip(project_near, "dp", 1)
+    rest_far = flip(rest_near, "dp", 1)
+
+    table = (place, pack_long, item_table, tau_table)
+    bias_own = ordered(project_bias, core)
+    bias_other = ordered(biases[: project_bias.size].reshape(project_bias.shape), core)
+    expand_all = jnp.concatenate([ordered(expand_bias, core), ordered(biases[project_bias.size :], core)])
+    vectors = jnp.stack(
+        [merge_bias, first_gain, first_shift, reduce_bias, second_gain, second_shift, merge_bias, merge_bias]
+    )
+    q0, k0, v0, o0, r0, p0 = attend(
+        *table, delta_table, inputs, project_weight, project_weight, bias_own, True
+    )
+    q1, k1, v1, o1, r1, p1 = attend(
+        *table, delta_table, inputs, project_near, project_far, bias_other, False
+    )
+    block_output, dh1, grad_att, grad_feed, sums, sum_hidden = feed(
+        place, o0, o1, inputs, grad_output, merge_weight, expand_weight, reduce_weight,
+        rest_near, rest_far, expand_all[None], vectors,
+    )
+    back0 = attend_back(*table, q0, k0, v0, grad_att, o0, r0, p0, 0)
+    back1 = attend_back(*table, q1, k1, v1, grad_att, o1, r1, p1, 1)
+    grads = tuple(back0) + tuple(back1)
+    grad_project, sum_project = project_grad(inputs, grads)
+    dx = input_grad(place, dh1, project_weight, project_near, project_far, grads)
+
+    feed_sum = sum_quarters(grad_feed.reshape(2, 2, *grad_feed.shape[1:]), dp_size)
+    project_sum = sum_quarters(grad_project, dp_size)
+
+    wide = sum_project.shape[1]
+    per_slot = [
+        jnp.concatenate(
+            [
+                sums[:6].reshape(-1),
+                ordered(sum_hidden[0, s * 2 * hid : (s + 1) * 2 * hid], core),
+                ordered(sum_project[2 * s : 2 * s + 2], core).reshape(-1),
+            ]
+        )
+        for s in (0, 1)
+    ]
+    small = per_slot[0] + flip(per_slot[1], "tensor", 1)
+    mask = 1
+    while mask < dp_size:
+        small = small + flip(small, "dp", mask)
+        mask *= 2
+    vec = small[: 6 * d].reshape(6, d)
+    hidden = small[6 * d : 6 * d + 2 * hid]
+    biases = small[6 * d + 2 * hid :].reshape(2, wide)
+
+    feed_sum = feed_sum.astype(F32)
+    project_sum = project_sum.astype(F32).reshape(2, 3, d, PAIR)
+    return (
+        block_output,
+        dx,
+        jnp.concatenate([project_sum[0], project_sum[1]], axis=-1),
+        biases,
+        feed_sum[:, hid + d :].reshape(2 * mrows, d),
+        vec[0],
+        vec[1],
+        vec[2],
+        jnp.concatenate([feed_sum[0, hid : hid + d], feed_sum[1, hid : hid + d]], axis=1),
+        hidden,
+        feed_sum[:, :hid].reshape(2 * hid, d),
+        vec[3],
+        vec[4],
+        vec[5],
+    )
+
+
+def on_device(*args, dp_size, tensor_size):
+    inputs, project_weight = args[0], args[5]
+    fits = tensor_size == 2 and dp_size >= 4 and dp_size & (dp_size - 1) == 0
+    fits = fits and inputs.shape[0] % LONG == 0 and project_weight.shape[2] == 2 * PAIR
+    if fits:
+        return row_layer(*args, dp_size=dp_size)
+    return split_layer(*args)
+
+
 def solution(mesh):
     placed = (
         P(("dp", "tensor"), None),
@@ -265,7 +877,9 @@
         P(("dp", "tensor"), None),
     )
     return jax.shard_map(
-        on_device,
+        functools.partial(
+            on_device, dp_size=mesh.shape["dp"], tensor_size=mesh.shape["tensor"]
+        ),
         mesh=mesh,
         in_specs=placed,
         out_specs=(

time: 1420 us -> 283 us (0.20)
  waiting for transfers between devices: 635 us -> 87 us
  matrix products: 497 us -> 0 us
  Pallas kernels: 0 us -> 135 us
  local copies, waits for them, and re-layouts: 112 us -> 16.8 us
  blocking collectives: 72.6 us -> 0 us
  other arithmetic: 76.9 us -> 14.1 us
  starting transfers between devices: 0.37 us -> 28 us
    dot_general x57 -> x0, matrix products: 497 us -> none  [the longest x6 92 us: one_block(): jnp.einsum('hqk,khd->qhd', lowered, block_k, preferred_element_type=jnp.f...]
    reduce_scatter x4 -> x0, waiting for transfers between devices: 386 us -> none  [the longest x1 111 us: on_device(): lax.psum_scatter(row_term(attended, merge_weight, 'tc,cd->td'), 'tensor',...]
    all_gather x4 -> x0, waiting for transfers between devices: 228 us -> none  [the longest x1 62.8 us: on_device(): lax.all_gather(grad_second.astype(jnp.bfloat16), 'tensor', axis=0, tiled=...]
    pallas_call x0 -> x7, Pallas kernels: none -> 135 us  [the longest x1 61.4 us: feed(): pl.pallas_call(functools.partial(feed_kernel, tiles=tiles, tile=tile), gr...]
    ppermute x0 -> x24, waiting for transfers between devices: none -> 87 us  [flip(): return lax.ppermute(v, axis, [(i, i ^ mask) for i in range(size)])]
    psum x2 -> x0, blocking collectives: 72.6 us -> none  [the longest x1 39.9 us: on_device(): lax.psum((grad_merge_bias, grad_gain_a, grad_shift_a, grad_reduce_bias, g...]
    reduce_sum x19 -> x0, other arithmetic: 51.8 us -> none  [the longest x6 18 us: one_block(): totals = jnp.sum(expo, axis=-1, keepdims=True)]
    while x30 -> x0, local copies, waits for them, and re-layouts: 38 us -> none  [the longest x3 22.7 us: attend_forward(): lax.map(one_block, split_blocks(shaped + (tau_row, delta_row, segment)))]
  transfers between devices with their start and end apart: 9 -> 24, of which waited for: 9 -> 13; matrix products, arithmetic and copies ran while one was open for 3% -> 7% of each run, Pallas kernels for 0% -> 26%
where the time goes in v1:
time: 283 us; the launch traced here: 282 us
  Pallas kernels  135 us (48%)
  waiting for transfers between devices  87 us (31%)
  starting transfers between devices  28 us (10%)
  local copies, waits for them, and re-layouts  16.8 us (6%)
  other arithmetic  14.1 us (5%)
    ppermute x24, waiting for transfers between devices, flip(): return lax.ppermute(v, axis, [(i, i ^ mask) for i in range(size)])  87 us
    pallas_call x1, Pallas kernels, feed(): pl.pallas_call(functools.partial(feed_kernel, tiles=tiles, tile=tile), gr...  61.4 us
    ppermute x24, starting transfers between devices, flip(): return lax.ppermute(v, axis, [(i, i ^ mask) for i in range(size)])  28 us
    pallas_call x2, Pallas kernels, attend_back(): pl.pallas_call(backward_kernel, grid_spec=pltpu.PrefetchScalarGridSpec(nu...  26.1 us
    pallas_call x2, Pallas kernels, attend(): pl.pallas_call(forward_kernel, grid_spec=pltpu.PrefetchScalarGridSpec(num...  26.1 us
    pallas_call x1, Pallas kernels, input_grad(): pl.pallas_call(input_grad_kernel, grid_spec=pltpu.PrefetchScalarGridSpec(...  11.3 us
    pallas_call x1, Pallas kernels, project_grad(): pl.pallas_call(project_grad_kernel, grid=(6,), in_specs=[whole(x.shape)]...  10.1 us
    convert_element_type x10, other arithmetic, add_low(): functools.reduce(lambda a, b: a + b, [p.astype(F32) for p in parts])  6.34 us
  transfers between devices with their start and end apart: 24, of which 13 were waited for; matrix products, arithmetic and copies ran while one was open for 7% of the time, Pallas kernels for 26%

profile of v1, /device:TPU:0, one launch (start us, length us, event | category | flops | bytes accessed | tf_op | source)
XLA Modules:
  0.0 282.0 jit_solution(5021244043856461754)
XLA Ops:
  1.7 3.0 %collective-permute-start = (bf16[3,512,128]{2,1,0:T(8,128)(2,1)S(1)}, bf16[3,512,128]{2,1,0:T(8,128)(2,1)S(1)}, u32[]{:S(2)}, u32[]{:S(2)}) collective-permute-start(bf16[3,512,128]{2,1,0:T(8,128)(2,1)S(1)} %constant_dynamic-slice_fusion.5), channel_id=1, source_target_pairs={{0,1},{1,0},{2,3},{3,2},{4,5},{5,4},{6,7},{7,6},{8,9},{9,8},{10,11... | collective-permute-start | bytes 1179656 | tf_op jit(solution)/shard_map/ppermute | solution.py:710
  8.4 2.1 collective-permute-start.3
  11.7 13.1 %attend_own.1 = (bf16[2304,256]{1,0:T(8,128)(2,1)}, bf16[2304,256]{1,0:T(8,128)(2,1)}, bf16[2304,256]{1,0:T(8,128)(2,1)}, bf16[2304,256]{1,0:T(8,128)(2,1)}, f32...) custom-call(s32[2]{0:T(128)} %pad_add_fusion.place, s32[12]{0:T(128)} %long_ref.7, s32[48]{0:T(128)} %item_ref.7, ...), custom_call_target="tpu_custom_call" | custom-call | flops 11000000512 | tf_op jit(solution)/shard_map/attend_own/pallas_call | solution.py:382
  25.7 13.5 %collective-permute-done.3.near_ref = bf16[1152,512]{1,0:T(8,128)(2,1)S(1)} collective-permute-done((bf16[1152,512]{1,0:T(8,128)(2,1)S(1)}, bf16[1152,512]{1,0:T(8,128)(2,1)S(1)}, u32[]{:S(2)}, u32[]{:S(2)}) %collective-permute-start.3) | collective-permute-done | bytes 1179680 | tf_op jit(solution)/shard_map/ppermute | solution.py:710
  41.3 13.0 %attend_other.1 = (bf16[2304,256]{1,0:T(8,128)(2,1)}, bf16[2304,256]{1,0:T(8,128)(2,1)}, bf16[2304,256]{1,0:T(8,128)(2,1)}, bf16[2304,256]{1,0:T(8,128)(2,1)}, f...) custom-call(s32[2]{0:T(128)} %pad_add_fusion.place, s32[12]{0:T(128)} %long_ref.7, s32[48]{0:T(128)} %item_ref.7, ...), custom_call_target="tpu_custom_call" | custom-call | flops 11000000512 | tf_op jit(solution)/shard_map/attend_other/pallas_call | solution.py:382
  55.3 61.4 %feed.1 = (f32[2304,512]{1,0:T(8,128)}, f32[2304,512]{1,0:T(8,128)}, bf16[2304,512]{1,0:T(8,128)(2,1)}, bf16[4,1152,512]{2,1,0:T(8,128)(2,1)}, f32[8,512]{1,0:T(8,128)}, /*index=5*/f32[8,2048]{1,0:T(8,128)}) custom-call(s32[2]{0:T(128)} %pad_add_fusion.place, bf16[2304,256]{1,0:T(8,128)(2,1)} %get-tuple-element.40.o0_ref.o_ref, ...), custom_call_target="tpu_custom_call" | custom-call | flops 60000002048 | tf_op jit(solution)/shard_map/feed/pallas_call | solution.py:528
  116.6 3.2 %slice_bitcast_fusion = bf16[2,1152,512]{2,1,0:T(8,128)(2,1)} fusion(bf16[2,2,1152,512]{3,2,1,0:T(8,128)(2,1)} %bitcast.80), kind=kLoop, calls=%fused_computation | loop fusion | bytes 4718592 | tf_op jit(solution)/shard_map/squeeze | solution.py:719
  120.3 13.1 %attend_back0.1 = (bf16[2304,256]{1,0:T(8,128)(2,1)}, bf16[2304,256]{1,0:T(8,128)(2,1)}, bf16[2304,256]{1,0:T(8,128)(2,1)}) custom-call(s32[2]{0:T(128)} %pad_add_fusion.place, s32[12]{0:T(128)} %long_ref.7, s32[48]{0:T(128)} %item_ref.7, f32[64]{0:T(128)} %tau_ref.7, bf16[2304,256]{1,0:T(8,128)(2,1)} %get-tuple-element.44.q_ref, ...), custom_call_target="tpu_custom_call" | custom-call | flops 11000000512 | tf_op jit(solution)/shard_map/attend_back0/pallas_call | solution.py:616
  133.4 13.0 %attend_back1.1 = (bf16[2304,256]{1,0:T(8,128)(2,1)}, bf16[2304,256]{1,0:T(8,128)(2,1)}, bf16[2304,256]{1,0:T(8,128)(2,1)}) custom-call(s32[2]{0:T(128)} %pad_add_fusion.place, s32[12]{0:T(128)} %long_ref.7, s32[48]{0:T(128)} %item_ref.7, f32[64]{0:T(128)} %tau_ref.7, bf16[2304,256]{1,0:T(8,128)(2,1)} %get-tuple-element.53.q_ref, ...), custom_call_target="tpu_custom_call" | custom-call | flops 11000000512 | tf_op jit(solution)/shard_map/attend_back1/pallas_call | solution.py:616
  146.4 10.1 %project_grad.1 = (bf16[2,2,1536,128]{3,2,1,0:T(8,128)(2,1)}, f32[8,256]{1,0:T(8,128)}) custom-call(bf16[2304,512]{1,0:T(8,128)(2,1)} %x_ref.7, bf16[2304,256]{1,0:T(8,128)(2,1)} %get-tuple-element.50.refs_0_, bf16[2304,256]{1,0:T(8,128)(2,1)} %get-tuple-element.51.refs_1_, bf16[2304,256]{1,0:T(8,128)(2,1)} %get-tuple-element.52.refs_2_, ...), custom_call_target="tpu_custom_call" | custom-call | flops 7000000000 | tf_op jit(solution)/shard_map/project_grad/pallas_call | solution.py:656
  158.7 1.7 fusion.1
  160.4 1.8 collective-permute-start.18
  164.5 1.8 collective-permute-start.6
  166.3 22.9 %collective-permute-done.18 = bf16[1152,512]{1,0:T(8,128)(2,1)S(1)} collective-permute-done((bf16[1152,512]{1,0:T(8,128)(2,1)S(1)}, bf16[1152,512]{1,0:T(8,128)(2,1)S(1)}, u32[]{:S(2)}, u32[]{:S(2)}) %collective-permute-start.18) | collective-permute-done | bytes 1179680 | tf_op jit(solution)/shard_map/ppermute | solution.py:710
  189.2 1.7 fusion.3
  191.1 1.8 collective-permute-start.19
  192.9 4.8 %collective-permute-done.6 = bf16[1536,128]{1,0:T(8,128)(2,1)S(1)} collective-permute-done((bf16[1536,128]{1,0:T(8,128)(2,1)S(1)}, bf16[1536,128]{1,0:T(8,128)(2,1)S(1)}, u32[]{:S(2)}, u32[]{:S(2)}) %collective-permute-start.6) | collective-permute-done | bytes 393248 | tf_op jit(solution)/shard_map/ppermute | solution.py:710
  198.9 1.8 collective-permute-start.7
  200.7 6.7 %collective-permute-done.19 = bf16[576,512]{1,0:T(8,128)(2,1)S(1)} collective-permute-done((bf16[576,512]{1,0:T(8,128)(2,1)S(1)}, bf16[576,512]{1,0:T(8,128)(2,1)S(1)}, u32[]{:S(2)}, u32[]{:S(2)}) %collective-permute-start.19) | collective-permute-done | bytes 589856 | tf_op jit(solution)/shard_map/ppermute | solution.py:710
  207.5 1.9 collective-permute-start.20
  209.9 1.8 collective-permute-start.8
  213.0 1.5 collective-permute-start.14
  214.6 2.2 collective-permute-done.14
  217.1 7.3 %collective-permute-done.15 = f32[4608]{0:T(1024)S(1)} collective-permute-done((f32[4608]{0:T(1024)S(1)}, f32[4608]{0:T(1024)S(1)}, u32[]{:S(2)}, u32[]{:S(2)}) %collective-permute-start.15) | collective-permute-done | bytes 18464 | tf_op jit(solution)/shard_map/ppermute | solution.py:710
  224.3 2.8 collective-permute-start.16
  227.5 2.9 %collective-permute-start.21 = (bf16[576,512]{1,0:T(8,128)(2,1)S(1)}, bf16[576,512]{1,0:T(8,128)(2,1)S(1)}, u32[]{:S(2)}, u32[]{:S(2)}) collective-permute-start(bf16[576,512]{1,0:T(8,128)(2,1)S(1)} %add_convert_fusion.1), channel_id=1, source_target_pairs={{0,16},{2,18},{4,20},{6,22},{8,24},{10,26},{12,28},{14,30},{16,0},... | collective-permute-start | bytes 1769480 | tf_op jit(solution)/shard_map/ppermute | solution.py:710
  230.4 11.3 %input_grad.1 = f32[2304,512]{1,0:T(8,128)} custom-call(s32[2]{0:T(128)} %pad_add_fusion.place, f32[2304,512]{1,0:T(8,128)} %get-tuple-element.43.dh1_ref, bf16[3,512,256]{2,1,0:T(8,128)(2,1)} %sa_ref.1, bf16[3,512,256]{2,1,0:T(8,128)(2,1)} %sa_ref.1, bf16[3,512,128]{2,1,0:T(8,128)(2,1)} %copy-done.13, bf16[3,512,128]{2,1,0:T(8,128)(2,1)} %copy-done.14, ...), custom_call_target="tpu_custom_call" | custom-call | flops 6000000000 | tf_op jit(solution)/shard_map/input_grad/pallas_call | solution.py:692
  241.7 2.9 %collective-permute-done.16 = f32[4608]{0:T(1024)S(1)} collective-permute-done((f32[4608]{0:T(1024)S(1)}, f32[4608]{0:T(1024)S(1)}, u32[]{:S(2)}, u32[]{:S(2)}) %collective-permute-start.16) | collective-permute-done | bytes 18464 | tf_op jit(solution)/shard_map/ppermute | solution.py:710
  245.2 3.6 %collective-permute-done.9 = bf16[768,128]{1,0:T(8,128)(2,1)S(1)} collective-permute-done((bf16[768,128]{1,0:T(8,128)(2,1)S(1)}, bf16[768,128]{1,0:T(8,128)(2,1)S(1)}, u32[]{:S(2)}, u32[]{:S(2)}) %collective-permute-start.9) | collective-permute-done | bytes 196640 | tf_op jit(solution)/shard_map/ppermute | solution.py:710
  250.4 9.7 %collective-permute-done.21 = bf16[576,512]{1,0:T(8,128)(2,1)S(1)} collective-permute-done((bf16[576,512]{1,0:T(8,128)(2,1)S(1)}, bf16[576,512]{1,0:T(8,128)(2,1)S(1)}, u32[]{:S(2)}, u32[]{:S(2)}) %collective-permute-start.21) | collective-permute-done | bytes 589856 | tf_op jit(solution)/shard_map/ppermute | solution.py:710
  260.2 1.6 collective-permute-start.22
  263.3 10.9 %collective-permute-done.22 = bf16[576,512]{1,0:T(8,128)(2,1)S(1)} collective-permute-done((bf16[576,512]{1,0:T(8,128)(2,1)S(1)}, bf16[576,512]{1,0:T(8,128)(2,1)S(1)}, u32[]{:S(2)}, u32[]{:S(2)}) %collective-permute-start.22) | collective-permute-done | bytes 589856 | tf_op jit(solution)/shard_map/ppermute | solution.py:710
  (115 shorter events, 29.8 us)
Async XLA Ops:
  1.7 23.9 %collective-permute-start = (bf16[3,512,128]{2,1,0:T(8,128)(2,1)S(1)}, bf16[3,512,128]{2,1,0:T(8,128)(2,1)S(1)}, u32[]{:S(2)}, u32[]{:S(2)}) collective-permute-start(bf16[3,512,128]{2,1,0:T(8,128)(2,1)S(1)} %constant_dynamic-slice_fusion.5), channel_id=1, source_target_pairs={{0,1},{1,0},{2,3},{3,2},{4,5},{5,4},{6,7},{7,6},{8,9},{9,8},{10,11... | collective-permute-start | bytes 1179656 | tf_op jit(solution)/shard_map/ppermute | solution.py:710
  6.1 19.5 %collective-permute-start.2 = (f32[1536]{0:T(1024)S(1)}, f32[1536]{0:T(1024)S(1)}, u32[]{:S(2)}, u32[]{:S(2)}) collective-permute-start(f32[1536]{0:T(1024)S(1)} %pad_maximum_fusion.5), channel_id=1, source_target_pairs={{0,1},{1,0},{2,3},{3,2},{4,5},{5,4},{6,7},{7,6},{8,9},{9,8},{10,11... | collective-permute-start | bytes 18440 | tf_op jit(solution)/shard_map/ppermute | solution.py:710
  8.4 30.9 %collective-permute-start.3 = (bf16[1152,512]{1,0:T(8,128)(2,1)S(1)}, bf16[1152,512]{1,0:T(8,128)(2,1)S(1)}, u32[]{:S(2)}, u32[]{:S(2)}) collective-permute-start(bf16[1152,512]{1,0:T(8,128)(2,1)S(1)} %pad_maximum_fusion.2), channel_id=1, source_target_pairs={{0,1},{1,0},{2,3},{3,2},{4,5},{5,4},{6,7},{7,6},{8,9},{9,8},{10,11... | collective-permute-start | bytes 3538952 | tf_op jit(solution)/shard_map/ppermute | solution.py:710
  11.6 13.3 %copy-start.2 = (f32[512]{0:T(512)S(1)}, f32[512]{0:T(512)}, u32[]{:S(2)}) copy-start(f32[512]{0:T(512)} %param.26) | copy-start | bytes 6148
  11.6 13.3 %copy-start.6 = (f32[512]{0:T(512)S(1)}, f32[512]{0:T(512)}, u32[]{:S(2)}) copy-start(f32[512]{0:T(512)} %param.27) | copy-start | bytes 6148
  11.6 13.3 %copy-start.7 = (f32[512]{0:T(512)S(1)}, f32[512]{0:T(512)}, u32[]{:S(2)}) copy-start(f32[512]{0:T(512)} %param.28) | copy-start | bytes 6148
  11.6 13.3 %copy-start.8 = (f32[512]{0:T(512)S(1)}, f32[512]{0:T(512)}, u32[]{:S(2)}) copy-start(f32[512]{0:T(512)} %param.32) | copy-start | bytes 6148
  11.7 13.3 %copy-start.9 = (f32[512]{0:T(512)S(1)}, f32[512]{0:T(512)}, u32[]{:S(2)}) copy-start(f32[512]{0:T(512)} %param.33) | copy-start | bytes 6148
  11.7 13.3 %copy-start.10 = (f32[512]{0:T(512)S(1)}, f32[512]{0:T(512)}, u32[]{:S(2)}) copy-start(f32[512]{0:T(512)} %param.34) | copy-start | bytes 6148
  25.6 14.9 %copy-start.13 = (bf16[3,512,128]{2,1,0:T(8,128)(2,1)}, bf16[3,512,128]{2,1,0:T(8,128)(2,1)S(1)}, u32[]{:S(2)}) copy-start(bf16[3,512,128]{2,1,0:T(8,128)(2,1)S(1)} %collective-permute-done.wa_ref.near_ref) | copy-start | bytes 1179652
  25.6 14.9 %collective-permute-start.1 = (bf16[3,512,128]{2,1,0:T(8,128)(2,1)S(1)}, bf16[3,512,128]{2,1,0:T(8,128)(2,1)S(1)}, u32[]{:S(2)}, u32[]{:S(2)}) collective-permute-start(bf16[3,512,128]{2,1,0:T(8,128)(2,1)S(1)} %collective-permute-done.wa_ref.near_ref), channel_id=1, source_target_pairs={{0,2},{2,0},{4,6},{6,4},{8,10},{10,8},{12,14},{14,12},{16,18},{18,... | collective-permute-start | bytes 1179656 | tf_op jit(solution)/shard_map/ppermute | solution.py:710
  39.3 15.0 %copy-start.11 = (bf16[1152,512]{1,0:T(8,128)(2,1)}, bf16[1152,512]{1,0:T(8,128)(2,1)S(1)}, u32[]{:S(2)}) copy-start(bf16[1152,512]{1,0:T(8,128)(2,1)S(1)} %collective-permute-done.3.near_ref) | copy-start | bytes 3538948
  39.3 15.0 %collective-permute-start.4 = (bf16[1152,512]{1,0:T(8,128)(2,1)S(1)}, bf16[1152,512]{1,0:T(8,128)(2,1)S(1)}, u32[]{:S(2)}, u32[]{:S(2)}) collective-permute-start(bf16[1152,512]{1,0:T(8,128)(2,1)S(1)} %collective-permute-done.3.near_ref), channel_id=1, source_target_pairs={{0,2},{2,0},{4,6},{6,4},{8,10},{10,8},{12,14},{14,12},{16,18},{18,... | collective-permute-start | bytes 3538952 | tf_op jit(solution)/shard_map/ppermute | solution.py:710
  119.8 38.8 %collective-permute-start.17 = (bf16[2,1152,512]{2,1,0:T(8,128)(2,1)}, bf16[2,1152,512]{2,1,0:T(8,128)(2,1)S(1)}, u32[]{:S(2)}, u32[]{:S(2)}) collective-permute-start(bf16[2,1152,512]{2,1,0:T(8,128)(2,1)} %slice_bitcast_fusion), channel_id=1, source_target_pairs={{0,2},{2,0},{4,6},{6,4},{8,10},{10,8},{12,14},{14,12},{16,18},{18,... | collective-permute-start | bytes 7077896 | tf_op jit(solution)/shard_map/ppermute | solution.py:710
  157.7 5.6 %collective-permute-start.5 = (bf16[2,1536,128]{2,1,0:T(8,128)(2,1)S(1)}, bf16[2,1536,128]{2,1,0:T(8,128)(2,1)}, u32[]{:S(2)}, u32[]{:S(2)}) collective-permute-start(bf16[2,1536,128]{2,1,0:T(8,128)(2,1)S(1)} %slice_bitcast_fusion.7), channel_id=1, source_target_pairs={{0,2},{2,0},{4,6},{6,4},{8,10},{10,8},{12,14},{14,12},{16,18},{18,... | collective-permute-start | bytes 2359304 | tf_op jit(solution)/shard_map/ppermute | solution.py:710
  160.4 28.8 %collective-permute-start.18 = (bf16[1152,512]{1,0:T(8,128)(2,1)S(1)}, bf16[1152,512]{1,0:T(8,128)(2,1)S(1)}, u32[]{:S(2)}, u32[]{:S(2)}) collective-permute-start(bf16[1152,512]{1,0:T(8,128)(2,1)S(1)} %fusion.1), channel_id=1, source_target_pairs={{0,1},{1,0},{2,3},{3,2},{4,5},{5,4},{6,7},{7,6},{8,9},{9,8},{10,11... | collective-permute-start | bytes 3538952 | tf_op jit(solution)/shard_map/ppermute | solution.py:710
  163.0 48.7 %collective-permute-start.12 = (f32[4608]{0:T(1024)S(1)}, f32[4608]{0:T(1024)S(1)}, u32[]{:S(2)}, u32[]{:S(2)}) collective-permute-start(f32[4608]{0:T(1024)S(1)} %fusion.10), channel_id=1, source_target_pairs={{0,1},{1,0},{2,3},{3,2},{4,5},{5,4},{6,7},{7,6},{8,9},{9,8},{10,11... | collective-permute-start | bytes 55304 | tf_op jit(solution)/shard_map/ppermute | solution.py:710
  164.5 33.2 %collective-permute-start.6 = (bf16[1536,128]{1,0:T(8,128)(2,1)S(1)}, bf16[1536,128]{1,0:T(8,128)(2,1)S(1)}, u32[]{:S(2)}, u32[]{:S(2)}) collective-permute-start(bf16[1536,128]{1,0:T(8,128)(2,1)S(1)} %fusion.5), channel_id=1, source_target_pairs={{0,1},{1,0},{2,3},{3,2},{4,5},{5,4},{6,7},{7,6},{8,9},{9,8},{10,11... | collective-permute-start | bytes 1179656 | tf_op jit(solution)/shard_map/ppermute | solution.py:710
  191.1 16.3 %collective-permute-start.19 = (bf16[576,512]{1,0:T(8,128)(2,1)S(1)}, bf16[576,512]{1,0:T(8,128)(2,1)S(1)}, u32[]{:S(2)}, u32[]{:S(2)}) collective-permute-start(bf16[576,512]{1,0:T(8,128)(2,1)S(1)} %constant_dynamic-slice_fusion), channel_id=1, source_target_pairs={{0,4},{2,6},{4,0},{6,2},{8,12},{10,14},{12,8},{14,10},{16,20},{18,... | collective-permute-start | bytes 1769480 | tf_op jit(solution)/shard_map/ppermute | solution.py:710
  198.9 11.0 %collective-permute-start.7 = (bf16[768,128]{1,0:T(8,128)(2,1)S(1)}, bf16[768,128]{1,0:T(8,128)(2,1)S(1)}, u32[]{:S(2)}, u32[]{:S(2)}) collective-permute-start(bf16[768,128]{1,0:T(8,128)(2,1)S(1)} %constant_dynamic-slice_fusion.1), channel_id=1, source_target_pairs={{0,4},{2,6},{4,0},{6,2},{8,12},{10,14},{12,8},{14,10},{16,20},{18,... | collective-permute-start | bytes 589832 | tf_op jit(solution)/shard_map/ppermute | solution.py:710
  207.5 19.8 %collective-permute-start.20 = (bf16[576,512]{1,0:T(8,128)(2,1)S(1)}, bf16[576,512]{1,0:T(8,128)(2,1)S(1)}, u32[]{:S(2)}, u32[]{:S(2)}) collective-permute-start(bf16[576,512]{1,0:T(8,128)(2,1)S(1)} %add_convert_fusion.2), channel_id=1, source_target_pairs={{0,8},{2,10},{4,12},{6,14},{8,0},{10,2},{12,4},{14,6},{16,24},{18,... | collective-permute-start | bytes 1769480 | tf_op jit(solution)/shard_map/ppermute | solution.py:710
  209.9 17.2 %collective-permute-start.8 = (bf16[768,128]{1,0:T(8,128)(2,1)S(1)}, bf16[768,128]{1,0:T(8,128)(2,1)S(1)}, u32[]{:S(2)}, u32[]{:S(2)}) collective-permute-start(bf16[768,128]{1,0:T(8,128)(2,1)S(1)} %add_convert_fusion.5), channel_id=1, source_target_pairs={{0,8},{2,10},{4,12},{6,14},{8,0},{10,2},{12,4},{14,6},{16,24},{18,... | collective-permute-start | bytes 589832 | tf_op jit(solution)/shard_map/ppermute | solution.py:710
  211.8 1.3 collective-permute-start.13
  213.0 3.8 %collective-permute-start.14 = (f32[4608]{0:T(1024)S(1)}, f32[4608]{0:T(1024)S(1)}, u32[]{:S(2)}, u32[]{:S(2)}) collective-permute-start(f32[4608]{0:T(1024)S(1)} %add.95), channel_id=1, source_target_pairs={{0,4},{2,6},{4,0},{6,2},{8,12},{10,14},{12,8},{14,10},{16,20},{18,... | collective-permute-start | bytes 55304 | tf_op jit(solution)/shard_map/ppermute | solution.py:710
  216.8 7.5 %collective-permute-start.15 = (f32[4608]{0:T(1024)S(1)}, f32[4608]{0:T(1024)S(1)}, u32[]{:S(2)}, u32[]{:S(2)}) collective-permute-start(f32[4608]{0:T(1024)S(1)} %add.96), channel_id=1, source_target_pairs={{0,8},{2,10},{4,12},{6,14},{8,0},{10,2},{12,4},{14,6},{16,24},{18,... | collective-permute-start | bytes 55304 | tf_op jit(solution)/shard_map/ppermute | solution.py:710
  224.3 20.3 %collective-permute-start.16 = (f32[4608]{0:T(1024)S(1)}, f32[4608]{0:T(1024)S(1)}, u32[]{:S(2)}, u32[]{:S(2)}) collective-permute-start(f32[4608]{0:T(1024)S(1)} %add.97), channel_id=1, source_target_pairs={{0,16},{2,18},{4,20},{6,22},{8,24},{10,26},{12,28},{14,30},{16,0},... | collective-permute-start | bytes 55304 | tf_op jit(solution)/shard_map/ppermute | solution.py:710
  227.2 21.6 %collective-permute-start.9 = (bf16[768,128]{1,0:T(8,128)(2,1)S(1)}, bf16[768,128]{1,0:T(8,128)(2,1)S(1)}, u32[]{:S(2)}, u32[]{:S(2)}) collective-permute-start(bf16[768,128]{1,0:T(8,128)(2,1)S(1)} %add_convert_fusion.4), channel_id=1, source_target_pairs={{0,16},{2,18},{4,20},{6,22},{8,24},{10,26},{12,28},{14,30},{16,0},... | collective-permute-start | bytes 589832 | tf_op jit(solution)/shard_map/ppermute | solution.py:710
  227.5 32.5 %collective-permute-start.21 = (bf16[576,512]{1,0:T(8,128)(2,1)S(1)}, bf16[576,512]{1,0:T(8,128)(2,1)S(1)}, u32[]{:S(2)}, u32[]{:S(2)}) collective-permute-start(bf16[576,512]{1,0:T(8,128)(2,1)S(1)} %add_convert_fusion.1), channel_id=1, source_target_pairs={{0,16},{2,18},{4,20},{6,22},{8,24},{10,26},{12,28},{14,30},{16,0},... | collective-permute-start | bytes 1769480 | tf_op jit(solution)/shard_map/ppermute | solution.py:710
  248.9 14.1 %collective-permute-start.10 = (bf16[768,128]{1,0:T(8,128)(2,1)S(1)}, bf16[768,128]{1,0:T(8,128)(2,1)S(1)}, u32[]{:S(2)}, u32[]{:S(2)}) collective-permute-start(bf16[768,128]{1,0:T(8,128)(2,1)S(1)} %add_convert_fusion.3), channel_id=1, source_target_pairs={{0,4},{2,6},{4,0},{6,2},{8,12},{10,14},{12,8},{14,10},{16,20},{18,... | collective-permute-start | bytes 589832 | tf_op jit(solution)/shard_map/ppermute | solution.py:710
  260.2 14.0 %collective-permute-start.22 = (bf16[576,512]{1,0:T(8,128)(2,1)S(1)}, bf16[576,512]{1,0:T(8,128)(2,1)S(1)}, u32[]{:S(2)}, u32[]{:S(2)}) collective-permute-start(bf16[576,512]{1,0:T(8,128)(2,1)S(1)} %add_convert_fusion), channel_id=1, source_target_pairs={{0,4},{2,6},{4,0},{6,2},{8,12},{10,14},{12,8},{14,10},{16,20},{18,... | collective-permute-start | bytes 1769480 | tf_op jit(solution)/shard_map/ppermute | solution.py:710
  263.1 11.7 %collective-permute-start.11 = (bf16[1536,128]{1,0:T(8,128)(2,1)S(1)}, bf16[1536,128]{1,0:T(8,128)(2,1)S(1)}, u32[]{:S(2)}, u32[]{:S(2)}) collective-permute-start(bf16[1536,128]{1,0:T(8,128)(2,1)S(1)} %maximum_select_fusion.5), channel_id=1, source_target_pairs={{0,2},{2,0},{4,6},{6,4},{8,10},{10,8},{12,14},{14,12},{16,18},{18,... | collective-permute-start | bytes 1179656 | tf_op jit(solution)/shard_map/ppermute | solution.py:710
  274.7 2.9 %collective-permute-start.23 = (bf16[1152,512]{1,0:T(8,128)(2,1)S(1)}, bf16[1152,512]{1,0:T(8,128)(2,1)S(1)}, u32[]{:S(2)}, u32[]{:S(2)}) collective-permute-start(bf16[1152,512]{1,0:T(8,128)(2,1)S(1)} %maximum_select_fusion.2), channel_id=1, source_target_pairs={{0,2},{2,0},{4,6},{6,4},{8,10},{10,8},{12,14},{14,12},{16,18},{18,... | collective-permute-start | bytes 3538952 | tf_op jit(solution)/shard_map/ppermute | solution.py:710
  (7 other events, 24.5 us)

commit v2 on v1

--- a/solution.py
+++ b/solution.py
@@ -4,13 +4,15 @@
 from jax import lax
 from jax.experimental import pallas as pl
 from jax.experimental.pallas import tpu as pltpu
-from jax.sharding import PartitionSpec as P
+from jax.sharding import Mesh, PartitionSpec as P
 
 HEAD = 64
 SHORT = 96
 LONG = 384
 TABLE = 64
 PAIR = 2 * HEAD
+SMALL = 128
+SMALL_PAIR = 32
 LOG2E = 1.4426950408889634
 F32 = jnp.float32
 BF16 = jnp.bfloat16
@@ -298,7 +300,7 @@
 
 
 def forward_kernel(
-    place, long_ref, item_ref, tau_ref, delta_ref, x_ref, wa_ref, wb_ref, b_ref,
+    place, long_ref, item_ref, tau_ref, delta_ref, x_ref, wa_ref, wb_ref, ba_ref, bb_ref,
     q_ref, k_ref, v_ref, o_ref, r_ref, p_ref, w_ref, bias_ref,
 ):
     step = pl.program_id(0)
@@ -312,9 +314,10 @@
     bias_ref[...] = pack_bias(longer, rows, delta_ref)
     tau = pack_tau(rows, tau_ref) * (HEAD**-0.5 * LOG2E)
     x = x_ref[...]
-    q = (mm(x, w_ref[0]) + b_ref[0:1]).astype(BF16)
+    b = jnp.concatenate([ba_ref[...], bb_ref[...]], axis=1)
+    q = (mm(x, w_ref[0]) + b[0:1]).astype(BF16)
     k = mm(x, w_ref[1]).astype(BF16)
-    v = (mm(x, w_ref[2]) + b_ref[1:2]).astype(BF16)
+    v = (mm(x, w_ref[2]) + b[1:2]).astype(BF16)
     q_ref[...] = q
     k_ref[...] = k
     v_ref[...] = v
@@ -363,12 +366,12 @@
     return pl.BlockSpec(memory_space=pltpu.SMEM)
 
 
-def kernel_params():
-    return pltpu.CompilerParams(vmem_limit_bytes=60 * 2**20)
+def kernel_params(mib):
+    return pltpu.CompilerParams(vmem_limit_bytes=mib * 2**20)
 
 
 def cost(us):
-    return pl.CostEstimate(flops=int(us * 1.0e9), bytes_accessed=0, transcendentals=0)
+    return pl.CostEstimate(flops=int(us * 1.0e6), bytes_accessed=0, transcendentals=0)
 
 
 def attend(place, long_, item, tau, delta, x, wa, wb, bias, own):
@@ -388,7 +391,7 @@
             + [
                 pl.BlockSpec((3, d, PAIR), pick(h), pipeline_mode=pl.Buffered(1)) for h in (0, 1)
             ]
-            + [whole(bias.shape)],
+            + [pl.BlockSpec((2, PAIR), lambda i, place, *_, h=h: (0, place[0] ^ h)) for h in (0, 1)],
             out_specs=[row(cols)] * 5
             + [pl.BlockSpec((1, heads, LONG, LONG), lambda i, *_: (i, 0, 0, 0))],
             scratch_shapes=[pltpu.VMEM((3, d, cols), BF16), pltpu.VMEM((LONG, LONG), F32)],
@@ -398,27 +401,22 @@
             jax.ShapeDtypeStruct((n, cols), F32),
             jax.ShapeDtypeStruct((packs, heads, LONG, LONG), BF16),
         ],
-        compiler_params=kernel_params(),
-        cost_estimate=cost(11),
+        compiler_params=kernel_params(60),
+        cost_estimate=cost(1 if own else 8000),
         name="attend_own" if own else "attend_other",
-    )(place, long_, item, tau, delta, x, wa, wb, bias)
+    )(place, long_, item, tau, delta, x, wa, wb, bias, bias)
 
 
 def gelu_parts(u):
-    z = jnp.abs(u)
-    t = 1.0 / (1.0 + (0.3275911 * 0.7071067811865476) * z)
-    e = jnp.exp2(u * u * (-0.5 * LOG2E))
-    poly = 0.5 * -1.453152027 + t * (0.5 * 1.061405429)
-    poly = 0.5 * -0.284496736 + t * (0.5 * 1.421413741 + t * poly)
-    tail = t * (0.5 * 0.254829592 + t * poly) * e
-    return jnp.where(u >= 0, 1.0 - tail, tail), e
+    phi = 0.5 + 0.5 * lax.erf(u * 0.7071067811865476)
+    return phi, jnp.exp2(u * u * (-0.5 * LOG2E))
 
 
 def feed_kernel(
     place, o0_ref, o1_ref, x_ref, gy_ref, mk_ref, ms_ref, ek_ref, es_ref, rk_ref, rs_ref,
-    near_ref, far_ref, be_ref, vec_ref,
-    out_ref, dh1_ref, do_ref, grad_ref, sum_ref, sbe_ref,
-    wm_ref, act_ref, du_ref, gp_ref, n1_ref, dh2_ref, dh1b_ref, o_ref, *, tiles, tile,
+    near_ref, far_ref, b0_ref, b1_ref, b2_ref, b3_ref, bm_ref, g1_ref, h1_ref, br_ref, g2_ref, h2_ref,
+    out_ref, dh1_ref, do_ref, act_ref, du_ref, n1_ref, dh2_ref, dh1b_ref, sum_ref, sbe_ref, send_ref,
+    wm_ref, act_all, du_all, gp_ref, n1_all, dh2_all, dh1b_all, o_all, *, tiles, tile,
 ):
     step = pl.program_id(0)
     d = x_ref.shape[1]
@@ -438,26 +436,32 @@
     @pl.when(step < tiles)
     def _():
         here = pl.ds(pl.multiple_of(step * tile, tile), tile)
-        bm, g1, b1, br, g2, b2 = [vec_ref[k:k + 1] for k in range(6)]
+        bm, g1, b1, br, g2, b2 = [ref[...] for ref in (bm_ref, g1_ref, h1_ref, br_ref, g2_ref, h2_ref)]
+        be = (b0_ref, b1_ref, b2_ref, b3_ref)
         o0, o1 = o0_ref[...], o1_ref[...]
-        o_ref[here, :half] = o0
-        o_ref[here, half:] = o1
+        o_all[here, :mrows] = o0[:, mrows:]
+        o_all[here, mrows:] = o1[:, mrows:]
         h1 = x_ref[...].astype(F32) + (mm(o0, wm_ref[:half]) + mm(o1, wm_ref[half:]) + bm)
         c = h1 - row_mean(h1)
         rs = lax.rsqrt(row_mean(c * c) + 1e-05)
         xh = c * rs
         n1 = xh * g1 + b1
         low = n1.astype(BF16)
-        n1_ref[here] = low
+        n1_ref[...] = low
+        n1_all[here] = low
         u = mm(low, expand[0][...])
         fed = n1 + br
         for k in range(4):
             later = mm(low, expand[k + 1][...]) if k < 3 else None
             at = slice(k * hid, (k + 1) * hid)
-            u = u + be_ref[0:1, at]
+            u = u + be[k][...]
             phi, e = gelu_parts(u)
             act = (u * phi).astype(BF16)
-            act_ref[here, at] = act
+            mine = slice(k // 2 * hid, (k // 2 + 1) * hid)
+            if k % 2 == 0:
+                act_ref[:, mine] = act
+            else:
+                act_all[here, mine] = act
             gp_ref[:, at] = (phi + u * (e * 0.3989422804014327)).astype(BF16)
             fed = fed + mm(act, reduce_[k][...])
             u = later
@@ -469,7 +473,8 @@
         gg = gy * g2
         dh2 = rs2 * ((gg - row_mean(gg)) - xh2 * row_mean(gg * xh2))
         dh2b = dh2.astype(BF16)
-        dh2_ref[here] = dh2b
+        dh2_ref[...] = dh2b
+        dh2_all[here] = dh2b
         dn = dh2
         sbe = []
         da = mm_nt(dh2b, reduce_[0][...])
@@ -477,7 +482,11 @@
             later = mm_nt(dh2b, reduce_[k + 1][...]) if k < 3 else None
             at = slice(k * hid, (k + 1) * hid)
             du = (da * gp_ref[:, at].astype(F32)).astype(BF16)
-            du_ref[here, at] = du
+            mine = slice(k // 2 * hid, (k // 2 + 1) * hid)
+            if k % 2 == 0:
+                du_ref[:, mine] = du
+            else:
+                du_all[here, mine] = du
             sbe.append(col_sum(du.astype(F32)))
             dn = dn + mm_nt(du, expand[k][...])
             da = later
@@ -485,7 +494,8 @@
         dh1 = rs * ((gg1 - row_mean(gg1)) - xh * row_mean(gg1 * xh))
         dh1_ref[...] = dh1
         dh1b = dh1.astype(BF16)
-        dh1b_ref[here] = dh1b
+        dh1b_ref[...] = dh1b
+        dh1b_all[here] = dh1b
         do_ref[...] = mm_nt(dh1b, wm_ref[...]).astype(BF16)
         sums = [col_sum(dh1), col_sum(dn * xh), col_sum(dn), col_sum(dh2), col_sum(gy * xh2), col_sum(gy)]
         sums = jnp.concatenate(sums + [jnp.zeros((2, d), F32)], axis=0)
@@ -501,18 +511,27 @@
             sum_ref[...] += sums
             sbe_ref[...] += sbe
 
-    for quarter in range(4):
-
-        @pl.when(step == tiles + quarter)
-        def _(quarter=quarter):
-            at = slice(quarter * hid, (quarter + 1) * hid)
-            om = slice(quarter * mrows, (quarter + 1) * mrows)
-            grad_ref[0, 0:hid] = mm_tn(act_ref[:, at], dh2_ref[...]).astype(BF16)
-            grad_ref[0, hid:hid + d] = mm_tn(n1_ref[...], du_ref[:, at]).astype(BF16)
-            grad_ref[0, hid + d:] = mm_tn(o_ref[:, om], dh1b_ref[...]).astype(BF16)
-
-
-def feed(place, o0, o1, x, gy, merge, expand, reduce_, near, far, be, vec):
+    for slot in range(2):
+
+        @pl.when(step == tiles + slot)
+        def _(slot=slot):
+            at = slice(slot * hid, (slot + 1) * hid)
+            om = slice(slot * mrows, (slot + 1) * mrows)
+            send_ref[0, 0:hid] = mm_tn(act_all[:, at], dh2_all[...]).astype(BF16)
+            send_ref[0, hid:hid + d] = mm_tn(n1_all[...], du_all[:, at]).astype(BF16)
+            rows = hid + d + mrows
+            send_ref[0, hid + d:rows] = mm_tn(o_all[:, om], dh1b_all[...]).astype(BF16)
+            send_ref[0, rows:] = small_rows(place[0] ^ 1, sum_ref[...], sbe_ref[...], slot, 1, hid)
+
+
+def small_rows(which, sums, sbe, slot, h, hid):
+    lo = (2 * slot + h) * hid
+    part = jnp.where(which == 0, sums[0:3], sums[3:6])
+    fill = jnp.zeros((SMALL - 4, sums.shape[1]), F32)
+    return jnp.concatenate([sbe[0:1, lo:lo + hid], part, fill], axis=0).astype(BF16)
+
+
+def feed(place, o0, o1, x, gy, merge, expand, reduce_, near, far, be0, be1, vecs):
     n, d = x.shape
     tile = LONG
     tiles = n // tile
@@ -524,148 +543,212 @@
     by_row = lambda shape, h: pl.BlockSpec(shape, lambda i, place: (place[0] ^ h, 0), pipeline_mode=once)
     by_col = lambda shape, h: pl.BlockSpec(shape, lambda i, place: (0, place[0] ^ h), pipeline_mode=once)
     S = jax.ShapeDtypeStruct
-    grows = hid + d + mrows
+    grows = hid + d + mrows + SMALL
+    bias = lambda h: pl.BlockSpec((1, hid), lambda i, place: (0, place[0] ^ h), pipeline_mode=once)
     return pl.pallas_call(
         functools.partial(feed_kernel, tiles=tiles, tile=tile),
         grid_spec=pltpu.PrefetchScalarGridSpec(
             num_scalar_prefetch=1,
-            grid=(tiles + 4,),
+            grid=(tiles + 2,),
             in_specs=[row(o0.shape[1]), row(o1.shape[1]), row(d), row(d)]
             + [by_row((mrows, d), h) for h in (0, 1)]
             + [by_col((d, hid), h) for h in (0, 1)]
             + [by_row((hid, d), h) for h in (0, 1)]
-            + [whole(near.shape), whole(far.shape), whole(be.shape), whole(vec.shape)],
-            out_specs=[row(d), row(d), row(d)]
+            + [whole(near.shape), whole(far.shape)]
+            + [bias(0), bias(1), bias(0), bias(1)]
+            + [whole((1, d))] * 6,
+            out_specs=[row(d), row(d), row(d), row(2 * hid), row(2 * hid), row(d), row(d), row(d)]
             + [
-                pl.BlockSpec((1, grows, d), lambda i, *_: (jnp.maximum(i - tiles, 0), 0, 0)),
                 pl.BlockSpec((8, d), lambda i, *_: (0, 0)),
                 pl.BlockSpec((8, full_hid), lambda i, *_: (0, 0)),
+                pl.BlockSpec((1, grows, d), lambda i, *_: (jnp.maximum(i - tiles, 0), 0, 0)),
             ],
             scratch_shapes=[
                 pltpu.VMEM((4 * mrows, d), BF16),
-                pltpu.VMEM((n, full_hid), BF16),
-                pltpu.VMEM((n, full_hid), BF16),
+                pltpu.VMEM((n, 2 * hid), BF16),
+                pltpu.VMEM((n, 2 * hid), BF16),
                 pltpu.VMEM((tile, full_hid), BF16),
                 pltpu.VMEM((n, d), BF16),
                 pltpu.VMEM((n, d), BF16),
                 pltpu.VMEM((n, d), BF16),
-                pltpu.VMEM((n, 4 * mrows), BF16),
+                pltpu.VMEM((n, 2 * mrows), BF16),
             ],
         ),
-        out_shape=[S((n, d), F32), S((n, d), F32), S((n, d), BF16), S((4, grows, d), BF16)]
-        + [S((8, d), F32), S((8, full_hid), F32)],
-        compiler_params=kernel_params(),
+        out_shape=[S((n, d), F32), S((n, d), F32), S((n, d), BF16)]
+        + [S((n, 2 * hid), BF16)] * 2
+        + [S((n, d), BF16)] * 3
+        + [S((8, d), F32), S((8, full_hid), F32), S((2, grows, d), BF16)],
+        compiler_params=kernel_params(58),
         cost_estimate=cost(60),
         name="feed",
-    )(place, o0, o1, x, gy, merge, merge, expand, expand, reduce_, reduce_, near, far, be, vec)
-
-
-def backward_kernel(
-    place, long_ref, item_ref, tau_ref, q_ref, k_ref, v_ref, g_ref, o_ref, r_ref, p_ref,
-    dq_ref, dk_ref, dv_ref,
+    )(place, o0, o1, x, gy, merge, merge, expand, expand, reduce_, reduce_, near, far, be0, be0, be1, be1, *vecs)
+
+
+def feed_grad_kernel(
+    place, act_hbm, du_hbm, n1_hbm, dh2_hbm, dh1b_hbm, o0_hbm, o1_hbm, sum_ref, sbe_ref, keep_hbm,
+    act, du, n1, dh2, dh1b, o, keep, sems, out_sems,
 ):
-    _, rows = pack_rows(pl.program_id(0) + place[1], long_ref, item_ref)
-    tau = pack_tau(rows, tau_ref) * HEAD**-0.5
-    heads = q_ref.shape[1] // HEAD
+    hid, d, mrows = act.shape[2], n1.shape[1], o.shape[2]
+
+    def fetch(src, dst, k):
+        copy = pltpu.make_async_copy(src, dst, sems.at[k])
+        copy.start()
+        return copy
+
+    cols = lambda s: (slice(None), pl.ds(s * hid, hid))
+    heads = lambda ref: ref.at[:, pl.ds(0, mrows)]
+    order = (
+        (act_hbm.at[cols(1)], act.at[1]), (dh2_hbm, dh2), (n1_hbm, n1), (du_hbm.at[cols(1)], du.at[1]),
+        (heads(o1_hbm), o.at[1]), (dh1b_hbm, dh1b),
+        (act_hbm.at[cols(0)], act.at[0]), (du_hbm.at[cols(0)], du.at[0]), (heads(o0_hbm), o.at[0]),
+    )
+    copies = [fetch(src, dst, k) for k, (src, dst) in enumerate(order)]
+    flush = []
+    rows = hid + d + mrows
+    for slot, waits in ((1, (0, 2, 4, 6)), (0, (6, 7, 8, 9))):
+        for k in range(waits[0], waits[1]):
+            copies[k].wait()
+        keep[slot, 0:hid] = mm_tn(act[slot], dh2[...]).astype(BF16)
+        for k in range(waits[1], waits[2]):
+            copies[k].wait()
+        keep[slot, hid:hid + d] = mm_tn(n1[...], du[slot]).astype(BF16)
+        for k in range(waits[2], waits[3]):
+            copies[k].wait()
+        keep[slot, hid + d:rows] = mm_tn(o[slot], dh1b[...]).astype(BF16)
+        keep[slot, rows:] = small_rows(place[0], sum_ref[...], sbe_ref[...], slot, 0, hid)
+        out = pltpu.make_async_copy(keep.at[slot], keep_hbm.at[slot], out_sems.at[slot])
+        out.start()
+        flush.append(out)
+    for out in flush:
+        out.wait()
+
+
+def feed_grad(place, act, du, n1, dh2, dh1b, o0, o1, sums, sbe):
+    n, d = n1.shape
+    hid, mrows = act.shape[1] // 2, o0.shape[1] // 2
+    grows = hid + d + mrows + SMALL
+    hbm = pl.BlockSpec(memory_space=pl.ANY)
+    return pl.pallas_call(
+        feed_grad_kernel,
+        in_specs=[smem()] + [hbm] * 7 + [whole(sums.shape), whole(sbe.shape)],
+        out_specs=hbm,
+        out_shape=jax.ShapeDtypeStruct((2, grows, d), BF16),
+        scratch_shapes=[
+            pltpu.VMEM((2, n, hid), BF16),
+            pltpu.VMEM((2, n, hid), BF16),
+            pltpu.VMEM((n, d), BF16),
+            pltpu.VMEM((n, d), BF16),
+            pltpu.VMEM((n, d), BF16),
+            pltpu.VMEM((2, n, mrows), BF16),
+            pltpu.VMEM((2, grows, d), BF16),
+            pltpu.SemaphoreType.DMA((9,)),
+            pltpu.SemaphoreType.DMA((2,)),
+        ],
+        compiler_params=kernel_params(58),
+        cost_estimate=cost(9),
+        name="feed_grad",
+    )(place, act, du, n1, dh2, dh1b, o0, o1, sums, sbe)
+
+
+def backward_kernel(place, long_ref, item_ref, tau_ref, *refs, sets, steps, group):
+    step = pl.program_id(0)
+    width = group * LONG
+    per = [refs[7 * s:7 * s + 7] for s in range(sets)]
+    x_ref = refs[7 * sets]
+    outs = refs[7 * sets + 1:7 * sets + 1 + 2 * sets]
+    x_all, d_all = refs[-2:]
+    x_all[pl.ds(pl.multiple_of(step * width, width), width)] = x_ref[...]
     lane = lax.broadcasted_iota(jnp.int32, (1, PAIR), 1)
     first = lane < HEAD
     ready = []
-    for i in range(heads // 2):
-        at = slice(i * PAIR, (i + 1) * PAIR)
-        g = g_ref[:, at].astype(F32) * r_ref[:, at]
-        low = g.astype(BF16)
-        scaled = (g * tau).astype(BF16).astype(F32)
-        d = scaled * o_ref[:, at].astype(F32)
-        v = v_ref[:, at].astype(F32)
-        for j in range(2):
-            own = first if j == 0 else jnp.logical_not(first)
-            spare = HEAD if j == 0 else 0
-            dd = jnp.sum(jnp.where(own, d, 0.0), axis=1, keepdims=True)
-            high = dd.astype(BF16).astype(F32)
-            left = jnp.where(lane == spare, -high, jnp.where(lane == spare + 1, high - dd, 0.0))
-            left = jnp.where(own, scaled, left).astype(BF16)
-            ones = jnp.where(jnp.logical_or(lane == spare, lane == spare + 1), 1.0, 0.0)
-            right = jnp.where(own, v, ones).astype(BF16)
-            ready.append((left, right, low[:, j * HEAD:(j + 1) * HEAD]))
-
-    def score(h):
-        return mm_nt(ready[h][0], ready[h][1])
-
+    for m in range(group):
+        _, rows = pack_rows(step * group + m + place[1], long_ref, item_ref)
+        tau = pack_tau(rows, tau_ref) * HEAD**-0.5
+        here = slice(m * LONG, (m + 1) * LONG)
+        for s in range(sets):
+            _, _, v_ref, g_ref, o_ref, r_ref, _ = per[s]
+            g = g_ref[here].astype(F32) * r_ref[here]
+            low = g.astype(BF16)
+            scaled = (g * tau).astype(BF16).astype(F32)
+            d = scaled * o_ref[here].astype(F32)
+            v = v_ref[here].astype(F32)
+            for j in range(2):
+                own = first if j == 0 else jnp.logical_not(first)
+                spare = HEAD if j == 0 else 0
+                dd = jnp.sum(jnp.where(own, d, 0.0), axis=1, keepdims=True)
+                high = dd.astype(BF16).astype(F32)
+                left = jnp.where(lane == spare, -high, jnp.where(lane == spare + 1, high - dd, 0.0))
+                left = jnp.where(own, scaled, left).astype(BF16)
+                ones = jnp.where(jnp.logical_or(lane == spare, lane == spare + 1), 1.0, 0.0)
+                right = jnp.where(own, v, ones).astype(BF16)
+                ready.append((left, right, low[:, j * HEAD:(j + 1) * HEAD], m, s, j))
     res = []
-    t = score(0)
-    for h in range(heads):
-        later = score(h + 1) if h + 1 < heads else None
-        at = slice(h * HEAD, (h + 1) * HEAD)
-        w = p_ref[0, h]
+    t = mm_nt(*ready[0][:2])
+    for n, (_, _, low, m, s, j) in enumerate(ready):
+        later = mm_nt(*ready[n + 1][:2]) if n + 1 < len(ready) else None
+        q_ref, k_ref, _, _, _, _, p_ref = per[s]
+        here = slice(m * LONG, (m + 1) * LONG)
+        at = slice(j * HEAD, (j + 1) * HEAD)
+        w = p_ref[m, j]
         r = (w.astype(F32) * t).astype(BF16)
-        res.append((mm(r, k_ref[:, at]), mm_tn(q_ref[:, at], r), mm_tn(ready[h][2], w)))
+        res.append((mm(r, k_ref[here, at]), mm_tn(q_ref[here, at], r), mm_tn(low, w)))
         t = later
-    for i in range(heads // 2):
-        at = slice(i * PAIR, (i + 1) * PAIR)
-        a, b = res[2 * i], res[2 * i + 1]
-        dq_ref[:, at] = jnp.concatenate([a[0], b[0]], axis=1).astype(BF16)
-        dk_ref[:, at] = jnp.concatenate([a[1], b[1]], axis=0).T.astype(BF16)
-        dv_ref[:, at] = jnp.concatenate([a[2], b[2]], axis=0).T.astype(BF16)
-
-
-def attend_back(place, long_, item, tau, q, k, v, g, o, r, p, slot):
-    n, cols = q.shape
-    packs = n // LONG
-    row = lambda c: pl.BlockSpec((LONG, c), lambda i, *_: (i, 0))
-    out = jax.ShapeDtypeStruct((n, cols), BF16)
+        if j == 1:
+            a, b = res[-2:]
+            out = [jnp.concatenate([a[0], b[0]], axis=1).astype(BF16)]
+            out += [jnp.concatenate([a[k], b[k]], axis=0).T.astype(BF16) for k in (1, 2)]
+            spot = pl.ds(pl.multiple_of(step * width + m * LONG, LONG), LONG)
+            for k in range(3):
+                outs[2 * s][here, k * PAIR:(k + 1) * PAIR] = out[k]
+                d_all[spot, (3 * s + k) * PAIR:(3 * s + k + 1) * PAIR] = out[k]
+
+    @pl.when(step == steps - 1)
+    def _():
+        depth = x_ref.shape[1]
+        res = mm_tn(x_all[...], d_all[...]).astype(BF16)
+        for s in range(sets):
+            grad_ref = outs[2 * s + 1]
+            for k in range(3):
+                grad_ref[k * depth:(k + 1) * depth] = res[:, (3 * s + k) * PAIR:(3 * s + k + 1) * PAIR]
+            cols = [slice((3 * s + k) * PAIR, (3 * s + k + 1) * PAIR) for k in (0, 2)]
+            dq, dv = [col_sum(d_all[:, at].astype(F32)) for at in cols]
+            small = jnp.concatenate([dq, dv, jnp.zeros((SMALL_PAIR - 2, PAIR), F32)], axis=0)
+            grad_ref[3 * depth:] = small.astype(BF16)
+
+
+def attend_back(place, long_, item, tau, saved, x, quarters):
+    n, d = x.shape
+    sets = len(quarters)
+    group = 2 // sets
+    width = group * LONG
+    steps = n // width
+    col = lambda c: pl.BlockSpec((width, PAIR), lambda i, *_: (i, c))
+    S = jax.ShapeDtypeStruct
+    rows = 3 * d + SMALL_PAIR
+    specs, operands = [], []
+    for slot, h in quarters:
+        p = saved[slot][-1]
+        specs += [col(h)] * 3 + [col(2 * slot + h)] + [col(h)] * 2
+        specs += [pl.BlockSpec((group, 2) + p.shape[2:], lambda i, *_, h=h: (i, h, 0, 0))]
+        operands += list(saved[slot])
     return pl.pallas_call(
-        backward_kernel,
+        functools.partial(backward_kernel, sets=sets, steps=steps, group=group),
         grid_spec=pltpu.PrefetchScalarGridSpec(
             num_scalar_prefetch=3,
-            grid=(packs,),
-            in_specs=[smem()]
-            + [row(cols)] * 3
-            + [pl.BlockSpec((LONG, cols), lambda i, *_: (i, slot))]
-            + [row(cols)] * 2
-            + [pl.BlockSpec((1,) + p.shape[1:], lambda i, *_: (i, 0, 0, 0))],
-            out_specs=[row(cols)] * 3,
+            grid=(steps,),
+            in_specs=[smem()] + specs + [pl.BlockSpec((width, d), lambda i, *_: (i, 0))],
+            out_specs=[
+                pl.BlockSpec((width, 3 * PAIR), lambda i, *_: (i, 0)),
+                pl.BlockSpec((rows, PAIR), lambda i, *_: (0, 0)),
+            ]
+            * sets,
+            scratch_shapes=[pltpu.VMEM((n, d), BF16), pltpu.VMEM((n, sets * 3 * PAIR), BF16)],
         ),
-        out_shape=[out] * 3,
-        compiler_params=kernel_params(),
-        cost_estimate=cost(11),
-        name="attend_back%d" % slot,
-    )(place, long_, item, tau, q, k, v, g, o, r, p)
-
-
-def project_grad_kernel(x_ref, *refs):
-    d_refs, (grad_ref, sum_ref) = refs[:-2], refs[-2:]
-    depth = x_ref.shape[1]
-    for k, d_ref in enumerate(d_refs):
-        slot, j = divmod(k, 3)
-
-        @pl.when(pl.program_id(0) == k)
-        def _(slot=slot, j=j, d_ref=d_ref):
-            d = d_ref[...]
-            res = mm_tn(x_ref[...], d).astype(BF16)
-            grad_ref[slot, 0, j * depth:(j + 1) * depth] = res[:, :PAIR]
-            grad_ref[slot, 1, j * depth:(j + 1) * depth] = res[:, PAIR:]
-            if j != 1:
-                row = slot * 2 + j // 2
-                sum_ref[row:row + 1] = col_sum(d.astype(F32))
-
-
-def project_grad(x, grads):
-    n, d = x.shape
-    cols = grads[0].shape[1]
-    S = jax.ShapeDtypeStruct
-    return pl.pallas_call(
-        project_grad_kernel,
-        grid=(6,),
-        in_specs=[whole(x.shape)] + [whole(g.shape) for g in grads],
-        out_specs=[
-            pl.BlockSpec((2, 2, 3 * d, PAIR), lambda i: (0, 0, 0, 0)),
-            pl.BlockSpec((8, cols), lambda i: (0, 0)),
-        ],
-        out_shape=[S((2, 2, 3 * d, PAIR), BF16), S((8, cols), F32)],
-        compiler_params=kernel_params(),
-        cost_estimate=cost(7),
-        name="project_grad",
-    )(x, *grads)
+        out_shape=[S((n, 3 * PAIR), BF16), S((rows, PAIR), BF16)] * sets,
+        compiler_params=kernel_params(60),
+        cost_estimate=cost(8),
+        name="attend_back_" + "_".join("%d%d" % q for q in quarters),
+    )(place, long_, item, tau, *operands, x)
 
 
 def input_grad_kernel(place, dh1_ref, ka_ref, sa_ref, near_ref, far_ref, *refs):
@@ -675,8 +758,7 @@
     def _():
         for j in range(3):
             for k, ref in enumerate((ka_ref, sa_ref, near_ref, far_ref)):
-                slot, h = divmod(k, 2)
-                lo = (slot * 3 + j) * 2 * PAIR + h * PAIR
+                lo = (k * 3 + j) * PAIR
                 w_ref[:, lo:lo + PAIR] = ref[j]
 
     d = jnp.concatenate([ref[...] for ref in d_refs], axis=1)
@@ -694,18 +776,18 @@
         grid_spec=pltpu.PrefetchScalarGridSpec(
             num_scalar_prefetch=1,
             grid=(n // tile,),
-            in_specs=[row(d), pick(0), pick(1), whole(near.shape), whole(far.shape)] + [row(cols)] * 6,
+            in_specs=[row(d), pick(0), pick(1), whole(near.shape), whole(far.shape)] + [row(cols)] * 4,
             out_specs=row(d),
-            scratch_shapes=[pltpu.VMEM((d, 6 * cols), BF16)],
+            scratch_shapes=[pltpu.VMEM((d, 4 * cols), BF16)],
         ),
         out_shape=jax.ShapeDtypeStruct((n, d), F32),
-        compiler_params=kernel_params(),
+        compiler_params=kernel_params(60),
         cost_estimate=cost(6),
         name="input_grad",
     )(place, dh1, weight, weight, near, far, *grads)
 
 
-def flip(v, axis, mask):
+def flip(v, axis, mask=1):
     size = lax.axis_size(axis)
     return lax.ppermute(v, axis, [(i, i ^ mask) for i in range(size)])
 
@@ -714,29 +796,12 @@
     return functools.reduce(lambda a, b: a + b, [p.astype(F32) for p in parts]).astype(BF16)
 
 
-def sum_quarters(grad, dp_size):
-    core = lax.axis_index("dp") % 2
-    got = flip(grad[:, 1], "dp", 1)
-    far = flip(add_low(grad[1, 0], got[1]), "tensor", 1)
-    mine = add_low(grad[0, 0], got[0], far)
-    rows = mine.shape[0] // 2
-    bit = lax.axis_index("dp") // 2 % 2
-    send = lax.dynamic_slice_in_dim(mine, (1 - bit) * rows, rows, 0)
-    keep = lax.dynamic_slice_in_dim(mine, bit * rows, rows, 0)
-    total = add_low(keep, flip(send, "dp", 2))
-    mask = 4
-    while mask < dp_size:
-        total = add_low(total, flip(total, "dp", mask))
-        mask *= 2
-    other = flip(total, "dp", 2)
-    total = jnp.where(bit == 0, jnp.concatenate([total, other]), jnp.concatenate([other, total]))
-    other = flip(total, "dp", 1)
-    return jnp.where(core == 0, jnp.stack([total, other]), jnp.stack([other, total]))
-
-
-def ordered(v, core):
-    cols = v.shape[-1] // 2
-    return jnp.where(core == 0, v, jnp.concatenate([v[..., cols:], v[..., :cols]], axis=-1))
+def piece(v, which, rows):
+    return lax.dynamic_slice_in_dim(v, which * rows, rows, v.ndim - 2)
+
+
+def in_order(bit, own, other):
+    return jnp.where(bit == 0, jnp.concatenate([own, other]), jnp.concatenate([other, own]))
 
 
 def row_layer(
@@ -758,16 +823,18 @@
     second_gain,
     second_shift,
     grad_output,
-    dp_size,
 ):
     n, d = inputs.shape
     hid = expand_weight.shape[1] // 2
     mrows = merge_weight.shape[0] // 2
-    core = lax.axis_index("dp") % 2
-    place = jnp.stack([core, lax.axis_index("tensor") * (n // LONG)]).astype(jnp.int32)
-
-    project_near = flip(lax.dynamic_slice_in_dim(project_weight, core * PAIR, PAIR, 2), "tensor", 1)
-    biases = flip(jnp.concatenate([project_bias.reshape(-1), expand_bias]), "tensor", 1)
+    core, side = lax.axis_index("core"), lax.axis_index("tensor")
+    outer = lax.axis_size("outer")
+    y_bit, z_bit = lax.axis_index("outer") % 2, lax.axis_index("outer") // 2 % 2
+    place = jnp.stack([core, side * (n // LONG)]).astype(jnp.int32)
+
+    split = project_bias.size
+    biases = flip(jnp.concatenate([project_bias.reshape(-1), expand_bias]), "tensor")
+    project_near = flip(lax.dynamic_slice_in_dim(project_weight, core * PAIR, PAIR, 2), "tensor")
     rest = jnp.concatenate(
         [
             lax.dynamic_slice_in_dim(expand_weight, core * hid, hid, 1),
@@ -776,90 +843,120 @@
         ],
         axis=0,
     )
-    rest_near = flip(rest, "tensor", 1)
-    project_far = flip(project_near, "dp", 1)
-    rest_far = flip(rest_near, "dp", 1)
+    rest_near = flip(rest, "tensor")
+    x, biases = lax.optimization_barrier((inputs, biases))
 
     table = (place, pack_long, item_table, tau_table)
-    bias_own = ordered(project_bias, core)
-    bias_other = ordered(biases[: project_bias.size].reshape(project_bias.shape), core)
-    expand_all = jnp.concatenate([ordered(expand_bias, core), ordered(biases[project_bias.size :], core)])
-    vectors = jnp.stack(
-        [merge_bias, first_gain, first_shift, reduce_bias, second_gain, second_shift, merge_bias, merge_bias]
-    )
     q0, k0, v0, o0, r0, p0 = attend(
-        *table, delta_table, inputs, project_weight, project_weight, bias_own, True
-    )
+        *table, delta_table, x, project_weight, project_weight, project_bias, True
+    )
+    project_near, o0 = lax.optimization_barrier((project_near, o0))
+    project_far = flip(project_near, "core")
     q1, k1, v1, o1, r1, p1 = attend(
-        *table, delta_table, inputs, project_near, project_far, bias_other, False
-    )
-    block_output, dh1, grad_att, grad_feed, sums, sum_hidden = feed(
+        *table, delta_table, inputs, project_near, project_far, biases[:split].reshape(project_bias.shape), False
+    )
+    rest_near, o1 = lax.optimization_barrier((rest_near, o1))
+    rest_far = flip(rest_near, "core")
+    block_output, dh1, grad_att, act, du, n1, dh2, dh1b, sums, sbe, send = feed(
         place, o0, o1, inputs, grad_output, merge_weight, expand_weight, reduce_weight,
-        rest_near, rest_far, expand_all[None], vectors,
-    )
-    back0 = attend_back(*table, q0, k0, v0, grad_att, o0, r0, p0, 0)
-    back1 = attend_back(*table, q1, k1, v1, grad_att, o1, r1, p1, 1)
-    grads = tuple(back0) + tuple(back1)
-    grad_project, sum_project = project_grad(inputs, grads)
-    dx = input_grad(place, dh1, project_weight, project_near, project_far, grads)
-
-    feed_sum = sum_quarters(grad_feed.reshape(2, 2, *grad_feed.shape[1:]), dp_size)
-    project_sum = sum_quarters(grad_project, dp_size)
-
-    wide = sum_project.shape[1]
-    per_slot = [
-        jnp.concatenate(
-            [
-                sums[:6].reshape(-1),
-                ordered(sum_hidden[0, s * 2 * hid : (s + 1) * 2 * hid], core),
-                ordered(sum_project[2 * s : 2 * s + 2], core).reshape(-1),
-            ]
-        )
-        for s in (0, 1)
-    ]
-    small = per_slot[0] + flip(per_slot[1], "tensor", 1)
-    mask = 1
-    while mask < dp_size:
-        small = small + flip(small, "dp", mask)
-        mask *= 2
-    vec = small[: 6 * d].reshape(6, d)
-    hidden = small[6 * d : 6 * d + 2 * hid]
-    biases = small[6 * d + 2 * hid :].reshape(2, wide)
-
-    feed_sum = feed_sum.astype(F32)
-    project_sum = project_sum.astype(F32).reshape(2, 3, d, PAIR)
+        rest_near, rest_far, expand_bias[None], biases[None, split:],
+        [v[None] for v in (merge_bias, first_gain, first_shift, reduce_bias, second_gain, second_shift)],
+    )
+    saved = ((q0, k0, v0, grad_att, o0, r0, p0), (q1, k1, v1, grad_att, o1, r1, p1))
+    back = lambda x, *quarters: attend_back(*table, saved, x, quarters)
+
+    got = flip(send, "core")
+    keep = feed_grad(place, act, du, n1, dh2, dh1b, o0, o1, sums, sbe)
+    got, keep = lax.optimization_barrier((got, keep))
+    part = keep.shape[1] // 2
+    half = part // 2
+    a, b = (keep[:, :part], got[:, :part]), (keep[:, part:], got[:, part:])
+    a_x = add_low(a[0][1], a[1][1])
+    b_y = add_low(*(piece(v, 1 - y_bit, half) for v in b))
+    x, a_x, b_y = lax.optimization_barrier((inputs, a_x, b_y))
+    a_x, b_y = flip(a_x, "tensor"), flip(b_y, "outer", 1)
+    d01, g01, d11, g11 = back(x, (0, 1), (1, 1))
+    got01, got11 = flip(g01, "core"), flip(g11, "core")
+    a_x, b_y, d11 = lax.optimization_barrier((a_x, b_y, d11))
+    a = add_low(a[0][0], a[1][0], a_x)
+    b = add_low(*(piece(v, y_bit, half) for v in b), b_y)
+    a_y, b_x = piece(a, 1 - y_bit, half), b[1]
+    x, a_y, b_x = lax.optimization_barrier((x, a_y, b_x))
+    a_y, b_x = flip(a_y, "outer", 1), flip(b_x, "tensor")
+    d10, g10 = back(x, (1, 0))
+    a_y, b_x, d10 = lax.optimization_barrier((a_y, b_x, d10))
+    far = add_low(g10, got11)
+    total = jnp.concatenate([add_low(piece(a, y_bit, half), a_y), add_low(b[0], b_x)])
+    to_z = piece(total, 1 - z_bit, half)
+    x, far, to_z = lax.optimization_barrier((x, far, to_z))
+    far, to_z = flip(far, "tensor"), flip(to_z, "outer", 2)
+    d00, g00 = back(x, (0, 0))
+    far, to_z, d00 = lax.optimization_barrier((far, to_z, d00))
+    feed_part = add_low(piece(total, z_bit, half), to_z)
+
+    mine = add_low(g00, got01, far)
+    rows = mine.shape[0] // 2
+    to_y = flip(piece(mine, 1 - y_bit, rows), "outer", 1)
+    if outer > 4:
+        came = flip(feed_part, "outer", 4)
+    project_part = add_low(piece(mine, y_bit, rows), to_y)
+    to_z = flip(project_part, "outer", 2)
+    d00, project_part = lax.optimization_barrier((d00, project_part))
+    dx = input_grad(place, dh1, project_weight, project_near, project_far, (d00, d01, d10, d11))
+    if outer > 4:
+        came, to_z, dx = lax.optimization_barrier((came, to_z, dx))
+        feed_part = add_low(feed_part, came)
+    project_part = add_low(project_part, to_z)
+    by_y, by_z = flip(feed_part, "outer", 1), flip(feed_part, "outer", 2)
+    if outer > 4:
+        project_part = add_low(project_part, flip(project_part, "outer", 4))
+    mid = half // 2
+    cross = jnp.concatenate([flip(by_z[:mid], "outer", 1), flip(by_y[mid:], "outer", 2)])
+    project_total = in_order(y_bit, project_part, flip(project_part, "outer", 1))
+    same = in_order(z_bit, feed_part, by_z)
+    other = in_order(z_bit, by_y, cross)
+    total = jnp.concatenate(
+        [in_order(y_bit, same[:half], other[:half]), in_order(y_bit, same[half:], other[half:])]
+    )
+    feed_sum = in_order(core, total[None], flip(total, "core")[None]).astype(F32)
+    project_sum = in_order(core, project_total[None], flip(project_total, "core")[None]).astype(F32)
+
+    weight = project_sum[:, : 3 * d].reshape(2, 3, d, PAIR)
+    small = feed_sum[:, hid + d + mrows :]
     return (
         block_output,
         dx,
-        jnp.concatenate([project_sum[0], project_sum[1]], axis=-1),
-        biases,
-        feed_sum[:, hid + d :].reshape(2 * mrows, d),
-        vec[0],
-        vec[1],
-        vec[2],
+        jnp.concatenate([weight[0], weight[1]], axis=-1),
+        jnp.concatenate([project_sum[0, 3 * d : 3 * d + 2], project_sum[1, 3 * d : 3 * d + 2]], axis=-1),
+        feed_sum[:, hid + d : hid + d + mrows].reshape(2 * mrows, d),
+        small[0, 1],
+        small[0, 2],
+        small[0, 3],
         jnp.concatenate([feed_sum[0, hid : hid + d], feed_sum[1, hid : hid + d]], axis=1),
-        hidden,
+        small[:, 0].reshape(-1),
         feed_sum[:, :hid].reshape(2 * hid, d),
-        vec[3],
-        vec[4],
-        vec[5],
-    )
-
-
-def on_device(*args, dp_size, tensor_size):
-    inputs, project_weight = args[0], args[5]
-    fits = tensor_size == 2 and dp_size >= 4 and dp_size & (dp_size - 1) == 0
-    fits = fits and inputs.shape[0] % LONG == 0 and project_weight.shape[2] == 2 * PAIR
-    if fits:
-        return row_layer(*args, dp_size=dp_size)
-    return split_layer(*args)
+        small[1, 1],
+        small[1, 2],
+        small[1, 3],
+    )
+
+
+def rows_fit(mesh):
+    size = mesh.shape["dp"]
+    return mesh.shape["tensor"] == 2 and size in (8, 16)
 
 
 def solution(mesh):
+    if rows_fit(mesh):
+        mesh = Mesh(mesh.devices.reshape(-1, 2, 2), ("outer", "core", "tensor"))
+        body, dp = row_layer, ("outer", "core")
+    else:
+        body, dp = split_layer, ("dp",)
+    all_ = P(dp + ("tensor",), None)
     placed = (
-        P(("dp", "tensor"), None),
-        P("dp"),
-        P("dp"),
+        all_,
+        P(dp),
+        P(dp),
         P(),
         P(),
         P(None, None, "tensor"),
@@ -874,17 +971,15 @@
         P(),
         P(),
         P(),
-        P(("dp", "tensor"), None),
+        all_,
     )
     return jax.shard_map(
-        functools.partial(
-            on_device, dp_size=mesh.shape["dp"], tensor_size=mesh.shape["tensor"]
-        ),
+        body,
         mesh=mesh,
         in_specs=placed,
         out_specs=(
-            P(("dp", "tensor"), None),
-            P(("dp", "tensor"), None),
+            all_,
+            all_,
             P(None, None, "tensor"),
             P(None, "tensor"),
             P("tensor", None),

time: 283 us -> 221 us (0.78)
  waiting for transfers between devices: 87 us -> 25.8 us
  other arithmetic: 14.1 us -> 17 us
    ppermute x24 -> x25, waiting for transfers between devices: 87 us -> 25.8 us  [flip(): return lax.ppermute(v, axis, [(i, i ^ mask) for i in range(size)])]
    pallas_call x1, Pallas kernels: 61.4 us -> 48.9 us  [feed(): pl.pallas_call(functools.partial(feed_kernel, tiles=tiles, tile=tile), gr...]
    pallas_call x3 -> x4, Pallas kernels: 36.2 us -> 47.7 us  [the longest x3 36.7 us: attend_back(): pl.pallas_call(functools.partial(backward_kernel, sets=sets, steps=steps,...]
    squeeze x2, local copies, waits for them, and re-layouts: 4.41 us -> 0.03 us  [the longest x1 0.02 us: row_layer(): a_y, b_x = (piece(a, 1 - y_bit, half), b[1])]
    convert_element_type x10 -> x13, other arithmetic: 6.34 us -> 9.83 us  [add_low(): functools.reduce(lambda a, b: a + b, [p.astype(F32) for p in parts])]
    unnamed x33 -> x25, local copies, waits for them, and re-layouts: 2.52 us -> 5.86 us
    ppermute x24 -> x25, starting transfers between devices: 28 us -> 25.8 us  [flip(): return lax.ppermute(v, axis, [(i, i ^ mask) for i in range(size)])]
  transfers between devices with their start and end apart: 24 -> 25, of which waited for: 13 -> 11; matrix products, arithmetic and copies ran while one was open for 7% -> 6% of each run, Pallas kernels for 26% -> 39%
where the time goes in v2:
time: 221 us; the launch traced here: 220 us
  Pallas kernels  134 us (61%)
  starting transfers between devices  25.8 us (12%)
  waiting for transfers between devices  25.8 us (12%)
  other arithmetic  17 us (8%)
  local copies, waits for them, and re-layouts  16.9 us (8%)
    pallas_call x1, Pallas kernels, feed(): pl.pallas_call(functools.partial(feed_kernel, tiles=tiles, tile=tile), gr...  48.9 us
    pallas_call x3, Pallas kernels, attend_back(): pl.pallas_call(functools.partial(backward_kernel, sets=sets, steps=steps,...  36.7 us
    pallas_call x2, Pallas kernels, attend(): pl.pallas_call(forward_kernel, grid_spec=pltpu.PrefetchScalarGridSpec(num...  26.1 us
    ppermute x25, waiting for transfers between devices, flip(): return lax.ppermute(v, axis, [(i, i ^ mask) for i in range(size)])  25.8 us
    ppermute x25, starting transfers between devices, flip(): return lax.ppermute(v, axis, [(i, i ^ mask) for i in range(size)])  25.8 us
    pallas_call x1, Pallas kernels, input_grad(): pl.pallas_call(input_grad_kernel, grid_spec=pltpu.PrefetchScalarGridSpec(...  11 us
    pallas_call x1, Pallas kernels, feed_grad(): pl.pallas_call(feed_grad_kernel, in_specs=[smem()] + [hbm] * 7 + [whole(s...  11 us
    convert_element_type x13, other arithmetic, add_low(): functools.reduce(lambda a, b: a + b, [p.astype(F32) for p in parts])  9.83 us
  transfers between devices with their start and end apart: 25, of which 11 were waited for; matrix products, arithmetic and copies ran while one was open for 6% of the time, Pallas kernels for 39%

profile of v2, /device:TPU:0, one launch (start us, length us, event | category | flops | bytes accessed | tf_op | source)
XLA Modules:
  0.0 220.3 jit_solution(18027253452930572442)
XLA Ops:
  1.7 3.0 %collective-permute-start = (bf16[3,512,128]{2,1,0:T(8,128)(2,1)S(1)}, bf16[3,512,128]{2,1,0:T(8,128)(2,1)S(1)}, u32[]{:S(2)}, u32[]{:S(2)}) collective-permute-start(bf16[3,512,128]{2,1,0:T(8,128)(2,1)S(1)} %constant_dynamic-slice_fusion.5), channel_id=1, source_target_pairs={{0,1},{1,0},{2,3},{3,2},{4,5},{5,4},{6,7},{7,6},{8,9},{9,8},{10,11... | collective-permute-start | bytes 1179656 | tf_op jit(solution)/shard_map/ppermute | solution.py:792
  7.5 2.1 collective-permute-start.2
  10.2 4.7 %collective-permute-done.1 = f32[1536]{0:T(1024)S(1)} collective-permute-done((f32[1536]{0:T(1024)S(1)}, f32[1536]{0:T(1024)S(1)}, u32[]{:S(2)}, u32[]{:S(2)}) %collective-permute-start.1) | collective-permute-done | bytes 6176 | tf_op jit(solution)/shard_map/ppermute | solution.py:792
  14.9 13.1 %attend_own.1 = (bf16[2304,256]{1,0:T(8,128)(2,1)}, bf16[2304,256]{1,0:T(8,128)(2,1)}, bf16[2304,256]{1,0:T(8,128)(2,1)}, bf16[2304,256]{1,0:T(8,128)(2,1)}, f32...) custom-call(s32[2]{0:T(128)} %pad_add_fusion.place, s32[12]{0:T(128)} %long_ref.9, s32[48]{0:T(128)} %item_ref.9, ...), custom_call_target="tpu_custom_call" | custom-call | flops 1000000 | tf_op jit(solution)/shard_map/attend_own/pallas_call | solution.py:385
  30.5 13.0 %attend_other.1 = (bf16[2304,256]{1,0:T(8,128)(2,1)}, bf16[2304,256]{1,0:T(8,128)(2,1)}, bf16[2304,256]{1,0:T(8,128)(2,1)}, bf16[2304,256]{1,0:T(8,128)(2,1)}, f...) custom-call(s32[2]{0:T(128)} %pad_add_fusion.place, s32[12]{0:T(128)} %long_ref.9, s32[48]{0:T(128)} %item_ref.9, ...), custom_call_target="tpu_custom_call" | custom-call | flops 8000000000 | tf_op jit(solution)/shard_map/attend_other/pallas_call | solution.py:385
  44.5 1.9 collective-permute-done.4.far_ref
  47.5 48.9 %feed.1 = (f32[2304,512]{1,0:T(8,128)}, f32[2304,512]{1,0:T(8,128)}, bf16[2304,512]{1,0:T(8,128)(2,1)}, bf16[2304,1024]{1,0:T(8,128)(2,1)}, bf16[2304,1024]{1,0:...) custom-call(s32[2]{0:T(128)} %pad_add_fusion.place, ...), custom_call_target="tpu_custom_call" | custom-call | flops 60000000 | tf_op jit(solution)/shard_map/feed/pallas_call | solution.py:548
  96.6 11.0 %feed_grad.1 = bf16[2,1280,512]{2,1,0:T(8,128)(2,1)} custom-call(s32[2]{0:T(128)} %pad_add_fusion.place, bf16[2304,1024]{1,0:T(8,128)(2,1)} %get-tuple-element.86.act_hbm, bf16[2304,1024]{1,0:T(8,128)(2,1)} %get-tuple-element.87.du_hbm, bf16[2304,512]{1,0:T(8,128)(2,1)} %get-tuple-element.88.n1_hbm, bf16[2304,512]{1,0:T(8,128)(2,1)} %get-tuple-element.89.dh2_hbm, ...), custom_call_target="tpu_custom_call" | custom-call | flops 9000000 | tf_op jit(solution)/shard_map/feed_grad/pallas_call | solution.py:631
  107.6 1.5 copy-done.5
  110.5 1.9 slice.130
  113.1 2.5 %fusion.3 = bf16[640,512]{1,0:T(8,128)(2,1)} fusion(bf16[2,1280,512]{2,1,0:T(8,128)(2,1)} %copy-done.5, bf16[2,1280,512]{2,1,0:T(8,128)(2,1)S(1)} %copy-done), kind=kLoop, calls=%fused_computation.21 | loop fusion | flops 1310720 | bytes 1966080 | tf_op jit(solution)/shard_map/convert_element_type | solution.py:796
  116.7 2.1 collective-permute-start.6
  118.8 1.5 collective-permute-start.7
  120.3 15.9 %attend_back_01_11.1 = (bf16[2304,384]{1,0:T(8,128)(2,1)}, bf16[1568,128]{1,0:T(8,128)(2,1)}, bf16[2304,384]{1,0:T(8,128)(2,1)}, bf16[1568,128]{1,0:T(8,128)(2,1)}) custom-call(s32[2]{0:T(128)} %pad_add_fusion.place, s32[12]{0:T(128)} %long_ref.9, s32[48]{0:T(128)} %item_ref.9, f32[64]{0:T(128)} %tau_ref.9, bf16[2304,256]{1,0:T(8,128)(2,1)} %get-tuple-element.97.refs_0_, ...), custom_call_target="tpu_custom_call" | custom-call | flops 8000000 | tf_op jit(solution)/shard_map/attend_back_01_11/pallas_call | solution.py:734
  137.2 1.7 fusion.1
  142.0 10.4 %attend_back_10.1 = (bf16[2304,384]{1,0:T(8,128)(2,1)}, bf16[1568,128]{1,0:T(8,128)(2,1)}) custom-call(s32[2]{0:T(128)} %pad_add_fusion.place, s32[12]{0:T(128)} %long_ref.9, s32[48]{0:T(128)} %item_ref.9, f32[64]{0:T(128)} %tau_ref.9, bf16[2304,256]{1,0:T(8,128)(2,1)} %get-tuple-element.103.refs_7_.refs_0_, ...), custom_call_target="tpu_custom_call" | custom-call | flops 8000000 | tf_op jit(solution)/shard_map/attend_back_10/pallas_call | solution.py:734
  155.6 1.6 collective-permute-start.12
  157.2 10.4 %attend_back_00.1 = (bf16[2304,384]{1,0:T(8,128)(2,1)}, bf16[1568,128]{1,0:T(8,128)(2,1)}) custom-call(s32[2]{0:T(128)} %pad_add_fusion.place, s32[12]{0:T(128)} %long_ref.9, s32[48]{0:T(128)} %item_ref.9, f32[64]{0:T(128)} %tau_ref.9, bf16[2304,256]{1,0:T(8,128)(2,1)} %get-tuple-element.97.refs_0_, bf16[2304,256]{1,0:T(8,128)(2,1)} %get-tuple-element.98.refs_1_, ...), custom_call_target="tpu_custom_call" | custom-call | flops 8000000 | tf_op jit(solution)/shard_map/attend_back_00/pallas_call | solution.py:734
  168.8 1.6 collective-permute-start.15
  170.8 2.7 %collective-permute-start.13 = (bf16[320,512]{1,0:T(8,128)(2,1)S(1)}, bf16[320,512]{1,0:T(8,128)(2,1)S(1)}, u32[]{:S(2)}, u32[]{:S(2)}) collective-permute-start(bf16[320,512]{1,0:T(8,128)(2,1)S(1)} %add_convert_fusion.6), channel_id=1, source_target_pairs={{0,16},{4,20},{8,24},{12,28},{16,0},{20,4},{24,8},{28,12},{1,17},{... | collective-permute-start | bytes 983048 | tf_op jit(solution)/shard_map/ppermute | solution.py:792
  173.5 2.5 %collective-permute-done.15 = bf16[784,128]{1,0:T(8,128)(2,1)S(1)} collective-permute-done((bf16[784,128]{1,0:T(8,128)(2,1)S(1)}, bf16[784,128]{1,0:T(8,128)(2,1)S(1)}, u32[]{:S(2)}, u32[]{:S(2)}) %collective-permute-start.15) | collective-permute-done | bytes 200736 | tf_op jit(solution)/shard_map/ppermute | solution.py:792
  176.6 11.0 %input_grad.1 = f32[2304,512]{1,0:T(8,128)} custom-call(s32[2]{0:T(128)} %pad_add_fusion.place, f32[2304,512]{1,0:T(8,128)} %get-tuple-element.128.dh1_ref, bf16[3,512,256]{2,1,0:T(8,128)(2,1)} %sa_ref.1, bf16[3,512,256]{2,1,0:T(8,128)(2,1)} %sa_ref.1, bf16[3,512,128]{2,1,0:T(8,128)(2,1)} %copy-done.10, bf16[3,512,128]{2,1,0:T(8,128)(2,1)} %copy-done.11, ...), custom_call_target="tpu_custom_call" | custom-call | flops 6000000 | tf_op jit(solution)/shard_map/input_grad/pallas_call | solution.py:774
  190.4 1.6 collective-permute-start.20
  192.1 1.5 collective-permute-start.21
  193.6 6.5 %collective-permute-done.17 = bf16[784,128]{1,0:T(8,128)(2,1)S(1)} collective-permute-done((bf16[784,128]{1,0:T(8,128)(2,1)S(1)}, bf16[784,128]{1,0:T(8,128)(2,1)S(1)}, u32[]{:S(2)}, u32[]{:S(2)}) %collective-permute-start.17) | collective-permute-done | bytes 200736 | tf_op jit(solution)/shard_map/ppermute | solution.py:792
  200.1 1.6 collective-permute-start.18
  201.7 1.5 collective-permute-done.20
  203.3 1.5 collective-permute-start.22
  205.4 2.7 %collective-permute-done.18 = bf16[784,128]{1,0:T(8,128)(2,1)S(1)} collective-permute-done((bf16[784,128]{1,0:T(8,128)(2,1)S(1)}, bf16[784,128]{1,0:T(8,128)(2,1)S(1)}, u32[]{:S(2)}, u32[]{:S(2)}) %collective-permute-start.18) | collective-permute-done | bytes 200736 | tf_op jit(solution)/shard_map/ppermute | solution.py:792
  208.3 2.3 %collective-permute-done.22 = bf16[160,512]{1,0:T(8,128)(2,1)S(1)} collective-permute-done((bf16[160,512]{1,0:T(8,128)(2,1)S(1)}, bf16[160,512]{1,0:T(8,128)(2,1)S(1)}, u32[]{:S(2)}, u32[]{:S(2)}) %collective-permute-start.22) | collective-permute-done | bytes 163872 | tf_op jit(solution)/shard_map/ppermute | solution.py:792
  215.3 1.5 slice.173
  218.9 1.5 pad_maximum_fusion
  (102 shorter events, 32.1 us)
Async XLA Ops:
  0.6 6.8 %copy-start.6 = (bf16[256,512]{1,0:T(8,128)(2,1)S(1)}, bf16[256,512]{1,0:T(8,128)(2,1)}, u32[]{:S(2)}) copy-start(bf16[256,512]{1,0:T(8,128)(2,1)} %ms_ref.1) | copy-start | bytes 786436
  1.7 26.2 %collective-permute-start = (bf16[3,512,128]{2,1,0:T(8,128)(2,1)S(1)}, bf16[3,512,128]{2,1,0:T(8,128)(2,1)S(1)}, u32[]{:S(2)}, u32[]{:S(2)}) collective-permute-start(bf16[3,512,128]{2,1,0:T(8,128)(2,1)S(1)} %constant_dynamic-slice_fusion.5), channel_id=1, source_target_pairs={{0,1},{1,0},{2,3},{3,2},{4,5},{5,4},{6,7},{7,6},{8,9},{9,8},{10,11... | collective-permute-start | bytes 1179656 | tf_op jit(solution)/shard_map/ppermute | solution.py:792
  6.1 8.7 %collective-permute-start.1 = (f32[1536]{0:T(1024)S(1)}, f32[1536]{0:T(1024)S(1)}, u32[]{:S(2)}, u32[]{:S(2)}) collective-permute-start(f32[1536]{0:T(1024)S(1)} %pad_maximum_fusion.4), channel_id=1, source_target_pairs={{0,1},{1,0},{2,3},{3,2},{4,5},{5,4},{6,7},{7,6},{8,9},{9,8},{10,11... | collective-permute-start | bytes 18440 | tf_op jit(solution)/shard_map/ppermute | solution.py:792
  7.5 36.0 %collective-permute-start.2 = (bf16[1152,512]{1,0:T(8,128)(2,1)S(1)}, bf16[1152,512]{1,0:T(8,128)(2,1)S(1)}, u32[]{:S(2)}, u32[]{:S(2)}) collective-permute-start(bf16[1152,512]{1,0:T(8,128)(2,1)S(1)} %pad_maximum_fusion.3), channel_id=1, source_target_pairs={{0,1},{1,0},{2,3},{3,2},{4,5},{5,4},{6,7},{7,6},{8,9},{9,8},{10,11... | collective-permute-start | bytes 3538952 | tf_op jit(solution)/shard_map/ppermute | solution.py:792
  28.0 1.8 copy-start.10
  28.0 1.8 collective-permute-start.3
  43.6 2.9 %copy-start.7 = (bf16[1152,512]{1,0:T(8,128)(2,1)}, bf16[1152,512]{1,0:T(8,128)(2,1)S(1)}, u32[]{:S(2)}) copy-start(bf16[1152,512]{1,0:T(8,128)(2,1)S(1)} %collective-permute-done.2.near_ref) | copy-start | bytes 3538948
  43.6 2.9 %collective-permute-start.4 = (bf16[1152,512]{1,0:T(8,128)(2,1)S(1)}, bf16[1152,512]{1,0:T(8,128)(2,1)S(1)}, u32[]{:S(2)}, u32[]{:S(2)}) collective-permute-start(bf16[1152,512]{1,0:T(8,128)(2,1)S(1)} %collective-permute-done.2.near_ref), channel_id=1, source_target_pairs={{0,2},{2,0},{1,3},{3,1},{4,6},{6,4},{5,7},{7,5},{8,10},{10,8},{9,1... | collective-permute-start | bytes 3538952 | tf_op jit(solution)/shard_map/ppermute | solution.py:792
  96.4 11.2 %collective-permute-start.5 = (bf16[2,1280,512]{2,1,0:T(8,128)(2,1)}, bf16[2,1280,512]{2,1,0:T(8,128)(2,1)S(1)}, u32[]{:S(2)}, u32[]{:S(2)}) collective-permute-start(bf16[2,1280,512]{2,1,0:T(8,128)(2,1)} %get-tuple-element.85), channel_id=1, source_target_pairs={{0,2},{2,0},{1,3},{3,1},{4,6},{6,4},{5,7},{7,5},{8,10},{10,8},{9,1... | collective-permute-start | bytes 7864328 | tf_op jit(solution)/shard_map/ppermute | solution.py:792
  110.5 5.2 %copy-start.1 = (bf16[2,640,512]{2,1,0:T(8,128)(2,1)}, bf16[2,640,512]{2,1,0:T(8,128)(2,1)S(1)}, u32[]{:S(2)}) copy-start(bf16[2,640,512]{2,1,0:T(8,128)(2,1)S(1)} %slice.129) | copy-start | bytes 3932164
  110.5 2.6 %copy-start = (bf16[2,1280,512]{2,1,0:T(8,128)(2,1)S(1)}, bf16[2,1280,512]{2,1,0:T(8,128)(2,1)}, u32[]{:S(2)}) copy-start(bf16[2,1280,512]{2,1,0:T(8,128)(2,1)} %feed_grad.1) | copy-start | bytes 7864324
  113.1 3.6 %copy-start.3 = (bf16[2,640,512]{2,1,0:T(8,128)(2,1)}, bf16[2,640,512]{2,1,0:T(8,128)(2,1)S(1)}, u32[]{:S(2)}) copy-start(bf16[2,640,512]{2,1,0:T(8,128)(2,1)S(1)} %slice.130) | copy-start | bytes 3932164
  116.7 19.6 %collective-permute-start.6 = (bf16[640,512]{1,0:T(8,128)(2,1)}, bf16[640,512]{1,0:T(8,128)(2,1)S(1)}, u32[]{:S(2)}, u32[]{:S(2)}) collective-permute-start(bf16[640,512]{1,0:T(8,128)(2,1)} %fusion.3), channel_id=1, source_target_pairs={{0,1},{1,0},{2,3},{3,2},{4,5},{5,4},{6,7},{7,6},{8,9},{9,8},{10,11... | collective-permute-start | bytes 1966088 | tf_op jit(solution)/shard_map/ppermute | solution.py:792
  118.8 17.5 %collective-permute-start.7 = (bf16[2,320,512]{2,1,0:T(8,128)(2,1)}, bf16[2,320,512]{2,1,0:T(8,128)(2,1)}, u32[]{:S(2)}, u32[]{:S(2)}) collective-permute-start(bf16[2,320,512]{2,1,0:T(8,128)(2,1)} %add_convert_fusion.1), channel_id=1, source_target_pairs={{0,4},{4,0},{8,12},{12,8},{16,20},{20,16},{24,28},{28,24},{1,5},{5... | collective-permute-start | bytes 1966088 | tf_op jit(solution)/shard_map/ppermute | solution.py:792
  136.3 16.1 %collective-permute-start.10 = (bf16[1568,128]{1,0:T(8,128)(2,1)}, bf16[1568,128]{1,0:T(8,128)(2,1)S(1)}, u32[]{:S(2)}, u32[]{:S(2)}) collective-permute-start(bf16[1568,128]{1,0:T(8,128)(2,1)} %get-tuple-element.119), channel_id=1, source_target_pairs={{0,2},{2,0},{1,3},{3,1},{4,6},{6,4},{5,7},{7,5},{8,10},{10,8},{9,1... | collective-permute-start | bytes 1204232 | tf_op jit(solution)/shard_map/ppermute | solution.py:792
  137.2 2.1 copy-start.4
  140.7 12.8 %collective-permute-start.8 = (bf16[320,512]{1,0:T(8,128)(2,1)S(1)}, bf16[320,512]{1,0:T(8,128)(2,1)S(1)}, u32[]{:S(2)}, u32[]{:S(2)}) collective-permute-start(bf16[320,512]{1,0:T(8,128)(2,1)S(1)} %constant_dynamic-slice_fusion.1), channel_id=1, source_target_pairs={{0,4},{4,0},{8,12},{12,8},{16,20},{20,16},{24,28},{28,24},{1,5},{5... | collective-permute-start | bytes 983048 | tf_op jit(solution)/shard_map/ppermute | solution.py:792
  141.3 12.2 %collective-permute-start.9 = (bf16[320,512]{1,0:T(8,128)(2,1)S(1)}, bf16[320,512]{1,0:T(8,128)(2,1)S(1)}, u32[]{:S(2)}, u32[]{:S(2)}) collective-permute-start(bf16[320,512]{1,0:T(8,128)(2,1)S(1)} %slice_bitcast_fusion.3), channel_id=1, source_target_pairs={{0,1},{1,0},{2,3},{3,2},{4,5},{5,4},{6,7},{7,6},{8,9},{9,8},{10,11... | collective-permute-start | bytes 983048 | tf_op jit(solution)/shard_map/ppermute | solution.py:792
  154.2 13.4 %collective-permute-start.11 = (bf16[1568,128]{1,0:T(8,128)(2,1)S(1)}, bf16[1568,128]{1,0:T(8,128)(2,1)S(1)}, u32[]{:S(2)}, u32[]{:S(2)}) collective-permute-start(bf16[1568,128]{1,0:T(8,128)(2,1)S(1)} %add_convert_fusion.4), channel_id=1, source_target_pairs={{0,1},{1,0},{2,3},{3,2},{4,5},{5,4},{6,7},{7,6},{8,9},{9,8},{10,11... | collective-permute-start | bytes 1204232 | tf_op jit(solution)/shard_map/ppermute | solution.py:792
  155.6 12.0 %collective-permute-start.14 = (bf16[1568,128]{1,0:T(8,128)(2,1)}, bf16[1568,128]{1,0:T(8,128)(2,1)S(1)}, u32[]{:S(2)}, u32[]{:S(2)}) collective-permute-start(bf16[1568,128]{1,0:T(8,128)(2,1)} %get-tuple-element.126), channel_id=1, source_target_pairs={{0,2},{2,0},{1,3},{3,1},{4,6},{6,4},{5,7},{7,5},{8,10},{10,8},{9,1... | collective-permute-start | bytes 1204232 | tf_op jit(solution)/shard_map/ppermute | solution.py:792
  155.6 12.0 %collective-permute-start.12 = (bf16[320,512]{1,0:T(8,128)(2,1)S(1)}, bf16[320,512]{1,0:T(8,128)(2,1)S(1)}, u32[]{:S(2)}, u32[]{:S(2)}) collective-permute-start(bf16[320,512]{1,0:T(8,128)(2,1)S(1)} %fusion.5), channel_id=1, source_target_pairs={{0,8},{4,12},{8,0},{12,4},{16,24},{20,28},{24,16},{28,20},{1,9},{5... | collective-permute-start | bytes 983048 | tf_op jit(solution)/shard_map/ppermute | solution.py:792
  168.8 7.2 %collective-permute-start.15 = (bf16[784,128]{1,0:T(8,128)(2,1)S(1)}, bf16[784,128]{1,0:T(8,128)(2,1)S(1)}, u32[]{:S(2)}, u32[]{:S(2)}) collective-permute-start(bf16[784,128]{1,0:T(8,128)(2,1)S(1)} %constant_dynamic-slice_fusion), channel_id=1, source_target_pairs={{0,4},{4,0},{8,12},{12,8},{16,20},{20,16},{24,28},{28,24},{1,5},{5... | collective-permute-start | bytes 602120 | tf_op jit(solution)/shard_map/ppermute | solution.py:792
  170.8 17.5 %collective-permute-start.13 = (bf16[320,512]{1,0:T(8,128)(2,1)S(1)}, bf16[320,512]{1,0:T(8,128)(2,1)S(1)}, u32[]{:S(2)}, u32[]{:S(2)}) collective-permute-start(bf16[320,512]{1,0:T(8,128)(2,1)S(1)} %add_convert_fusion.6), channel_id=1, source_target_pairs={{0,16},{4,20},{8,24},{12,28},{16,0},{20,4},{24,8},{28,12},{1,17},{... | collective-permute-start | bytes 983048 | tf_op jit(solution)/shard_map/ppermute | solution.py:792
  176.0 13.3 %collective-permute-start.16 = (bf16[784,128]{1,0:T(8,128)(2,1)S(1)}, bf16[784,128]{1,0:T(8,128)(2,1)S(1)}, u32[]{:S(2)}, u32[]{:S(2)}) collective-permute-start(bf16[784,128]{1,0:T(8,128)(2,1)S(1)} %add_convert_fusion.10), channel_id=1, source_target_pairs={{0,8},{4,12},{8,0},{12,4},{16,24},{20,28},{24,16},{28,20},{1,9},{5... | collective-permute-start | bytes 602120 | tf_op jit(solution)/shard_map/ppermute | solution.py:792
  189.4 10.7 %collective-permute-start.17 = (bf16[784,128]{1,0:T(8,128)(2,1)S(1)}, bf16[784,128]{1,0:T(8,128)(2,1)S(1)}, u32[]{:S(2)}, u32[]{:S(2)}) collective-permute-start(bf16[784,128]{1,0:T(8,128)(2,1)S(1)} %add_convert_fusion.9), channel_id=1, source_target_pairs={{0,16},{4,20},{8,24},{12,28},{16,0},{20,4},{24,8},{28,12},{1,17},{... | collective-permute-start | bytes 602120 | tf_op jit(solution)/shard_map/ppermute | solution.py:792
  190.4 12.8 %collective-permute-start.20 = (bf16[320,512]{1,0:T(8,128)(2,1)S(1)}, bf16[320,512]{1,0:T(8,128)(2,1)S(1)}, u32[]{:S(2)}, u32[]{:S(2)}) collective-permute-start(bf16[320,512]{1,0:T(8,128)(2,1)S(1)} %add_convert_fusion.5), channel_id=1, source_target_pairs={{0,8},{4,12},{8,0},{12,4},{16,24},{20,28},{24,16},{28,20},{1,9},{5... | collective-permute-start | bytes 983048 | tf_op jit(solution)/shard_map/ppermute | solution.py:792
  192.1 12.7 %collective-permute-start.21 = (bf16[320,512]{1,0:T(8,128)(2,1)S(1)}, bf16[320,512]{1,0:T(8,128)(2,1)S(1)}, u32[]{:S(2)}, u32[]{:S(2)}) collective-permute-start(bf16[320,512]{1,0:T(8,128)(2,1)S(1)} %add_convert_fusion.5), channel_id=1, source_target_pairs={{0,4},{4,0},{8,12},{12,8},{16,20},{20,16},{24,28},{28,24},{1,5},{5... | collective-permute-start | bytes 983048 | tf_op jit(solution)/shard_map/ppermute | solution.py:792
  200.1 7.9 %collective-permute-start.18 = (bf16[784,128]{1,0:T(8,128)(2,1)S(1)}, bf16[784,128]{1,0:T(8,128)(2,1)S(1)}, u32[]{:S(2)}, u32[]{:S(2)}) collective-permute-start(bf16[784,128]{1,0:T(8,128)(2,1)S(1)} %add_convert_fusion.8), channel_id=1, source_target_pairs={{0,4},{4,0},{8,12},{12,8},{16,20},{20,16},{24,28},{28,24},{1,5},{5... | collective-permute-start | bytes 602120 | tf_op jit(solution)/shard_map/ppermute | solution.py:792
  203.3 7.3 %collective-permute-start.22 = (bf16[160,512]{1,0:T(8,128)(2,1)S(1)}, bf16[160,512]{1,0:T(8,128)(2,1)S(1)}, u32[]{:S(2)}, u32[]{:S(2)}) collective-permute-start(bf16[160,512]{1,0:T(8,128)(2,1)S(1)} %slice.161), channel_id=1, source_target_pairs={{0,4},{4,0},{8,12},{12,8},{16,20},{20,16},{24,28},{28,24},{1,5},{5... | collective-permute-start | bytes 491528 | tf_op jit(solution)/shard_map/ppermute | solution.py:792
  204.8 5.8 %collective-permute-start.23 = (bf16[160,512]{1,0:T(8,128)(2,1)S(1)}, bf16[160,512]{1,0:T(8,128)(2,1)S(1)}, u32[]{:S(2)}, u32[]{:S(2)}) collective-permute-start(bf16[160,512]{1,0:T(8,128)(2,1)S(1)} %slice.162), channel_id=1, source_target_pairs={{0,8},{4,12},{8,0},{12,4},{16,24},{20,28},{24,16},{28,20},{1,9},{5... | collective-permute-start | bytes 491528 | tf_op jit(solution)/shard_map/ppermute | solution.py:792
  208.2 3.6 %collective-permute-start.19 = (bf16[1568,128]{1,0:T(8,128)(2,1)S(1)}, bf16[1568,128]{1,0:T(8,128)(2,1)S(1)}, u32[]{:S(2)}, u32[]{:S(2)}) collective-permute-start(bf16[1568,128]{1,0:T(8,128)(2,1)S(1)} %maximum_select_fusion.7), channel_id=1, source_target_pairs={{0,2},{2,0},{1,3},{3,1},{4,6},{6,4},{5,7},{7,5},{8,10},{10,8},{9,1... | collective-permute-start | bytes 1204232 | tf_op jit(solution)/shard_map/ppermute | solution.py:792
  211.6 3.1 %collective-permute-start.24 = (bf16[1280,512]{1,0:T(8,128)(2,1)S(1)}, bf16[1280,512]{1,0:T(8,128)(2,1)S(1)}, u32[]{:S(2)}, u32[]{:S(2)}) collective-permute-start(bf16[1280,512]{1,0:T(8,128)(2,1)S(1)} %get-tuple-element.151), channel_id=1, source_target_pairs={{0,2},{2,0},{1,3},{3,1},{4,6},{6,4},{5,7},{7,5},{8,10},{10,8},{9,1... | collective-permute-start | bytes 3932168 | tf_op jit(solution)/shard_map/ppermute | solution.py:792
  (5 other events, 5.8 us)
